TPU v7x, 32 devices: a whole 2x2x4 slice. The times are simulated.
32 devices in a mesh: stream: 2 (over y), page: 16 (over z, x, core).
Axes of the slice: x: 2, y: 2, z: 4, core: 2. Of those that a mesh axis runs over, the one named last changes fastest.
Arguments:
- block_input: bfloat16 [2, 9216, 768], P('stream', 'page'), may hold values from -6 to 6
- cotangent: bfloat16 [2, 9216, 768], P('stream', 'page'), may hold values from -6 to 6
- norm_gain: float32 [2, 768, 3], P('stream'), may hold values from 0.5 to 1.5
- norm_bias: float32 [2, 768, 3], P('stream'), may hold values from -2 to 2
- w_qkv: bfloat16 [2, 768, 2304], P('stream'), may hold values from -0.21875 to 0.21875
- w_out: bfloat16 [2, 768, 768], P('stream'), may hold values from -0.625 to 0.625
- w_query: bfloat16 [2, 768, 768], P('stream'), may hold values from -0.21875 to 0.21875
- w_keyval: bfloat16 [2, 768, 1536], P('stream'), may hold values from -0.21875 to 0.21875
- w_cross: bfloat16 [2, 768, 768], P('stream'), may hold values from -0.875 to 0.875
- w_up: bfloat16 [2, 768, 3072], P('stream'), may hold values from -0.21875 to 0.21875
- b_up: float32 [2, 3072], P('stream'), may hold values from -3 to 3
- w_down: bfloat16 [2, 3072, 768], P('stream'), may hold values from -0.109375 to 0.109375
- b_down: float32 [2, 768], P('stream'), may hold values from -2 to 2
- row_page: int32 [192], replicated, may hold values from 0 to 3, never falling along the last dimension, each value on 1 to 96 neighbouring positions
- lengths: int32 [16], P('page'), may hold values from 1 to 576, 4608 in all
Outputs:
- block_output: bfloat16 [2, 9216, 768], P('stream', 'page')
- input_grad: bfloat16 [2, 9216, 768], P('stream', 'page')
- gain_grad: float32 [2, 768, 3], P('stream', 'page')
- bias_grad: float32 [2, 768, 3], P('stream', 'page')
- qkv_grad: float32 [2, 768, 2304], P('stream', 'page')
- out_grad: float32 [2, 768, 768], P('stream', 'page')
- query_grad: float32 [2, 768, 768], P('stream', 'page')
- keyval_grad: float32 [2, 768, 1536], P('stream', 'page')
- cross_grad: float32 [2, 768, 768], P('stream', 'page')
- up_grad: float32 [2, 768, 3072], P('stream', 'page')
- up_bias_grad: float32 [2, 3072], P('stream', 'page')
- down_grad: float32 [2, 3072, 768], P('stream', 'page')
- down_bias_grad: float32 [2, 768], P('stream', 'page')
Inputs may be any that keep to these rules, and one draw needn't show every extreme that they name: `row_page`: page numbers never fall along the rows; each page has 1 to (96) rows and one has exactly (96). The lengths sum to 4608 and the longest is 576.
All inputs are finite; a program needn't handle non-finite values. No bound on the sum of `lengths` on one device may be relied on, other than what follows from the above.
Results may differ from a plain program's by a relative error of at most 0.019.
Values may be sent and summed in bfloat16 or wider, within the bound.
No kernel may reach another device: no remote copies, remote signals or barrier semaphores. Data moves between devices by JAX's collectives and lax.ppermute only.
A program may use at most 256 MiB of HBM per device.

v0:
```python
from functools import partial

import jax
import jax.numpy as jnp
from jax import lax
from jax.sharding import PartitionSpec as P

HEADS = 12
HEAD = 64
WIN = 12
SHIFT = 6


norm_eps = 1e-05
masked_score = -1e30


def extended_2(x, sides, width):
    for axis, dim in sides:
        size, length = (lax.axis_size(axis), x.shape[dim])
        up = [(i, (i + 1) % size) for i in range(size)]
        down = [(j, i) for i, j in up]
        last = lax.slice_in_dim(x, length - width, length, axis=dim)
        leading = lax.slice_in_dim(x, 0, width, axis=dim)
        before = lax.ppermute(last, axis, up)
        after = lax.ppermute(leading, axis, down)
        x = jnp.concatenate([before, x, after], axis=dim)
    return x


def from_partner(block, axis, apart):
    count = lax.axis_size(axis)
    route = []
    for low in range(count):
        high = low | 1 << apart
        if high != low and high < count:
            route += [(low, high), (high, low)]
    return lax.ppermute(block, axis, route)


def layer_norm(inputs, scales, shifts):
    average = jnp.mean(inputs, axis=1, keepdims=True)
    centred = inputs - average
    spread = jnp.mean(centred * centred, axis=1, keepdims=True)
    inverse = lax.rsqrt(spread + norm_eps)
    unit = centred * inverse
    return (unit * scales + shifts, unit, inverse)


def norm_back(upstream, unit, inverse, scales):
    scaled = upstream * scales
    inner = (
        scaled
        - jnp.mean(scaled, axis=1, keepdims=True)
        - unit * jnp.mean(scaled * unit, axis=1, keepdims=True)
    )
    return (inverse * inner, jnp.sum(upstream * unit, axis=0), jnp.sum(upstream, axis=0))


def transpose_dot(left, right):
    return lax.dot_general(
        left, right, (((0,), (0,)), ((), ())), preferred_element_type=jnp.float32
    )


def dot_back(left, right):
    return lax.dot_general(
        left, right, (((1,), (1,)), ((), ())), preferred_element_type=jnp.float32
    )


def head_slice(values, head):
    return lax.dynamic_slice_in_dim(values, head * HEAD, HEAD, 1)


def head_scores(queries, key_part, allowed, head):
    query_head = head_slice(queries, head)
    key_head = head_slice(key_part, head)
    scores = dot_back(query_head, key_head) * HEAD ** (-0.5)
    return (jnp.where(allowed, scores, masked_score), query_head, key_head)


def attend_forward(queries, key_part, value_part, allowed):
    row_count = queries.shape[0]

    def per_head(head, carried):
        mixed, log_total = carried
        scores, query_head, key_head = head_scores(queries, key_part, allowed, head)
        peak = jnp.max(scores, axis=1, keepdims=True)
        weights = jnp.exp(scores - peak)
        total = jnp.sum(weights, axis=1, keepdims=True)
        probs = (weights / total).astype(jnp.bfloat16)
        result = jnp.dot(probs, head_slice(value_part, head), preferred_element_type=jnp.float32)
        mixed = lax.dynamic_update_slice_in_dim(mixed, result, head * HEAD, 1)
        log_total = lax.dynamic_update_slice_in_dim(log_total, peak + jnp.log(total), head, 1)
        return (mixed, log_total)

    start = (
        jnp.zeros((row_count, queries.shape[1]), jnp.float32),
        jnp.zeros((row_count, HEADS), jnp.float32),
    )
    return lax.fori_loop(0, HEADS, per_head, start)


def attend_backward(queries, key_part, value_part, allowed, log_total, grad_mixed):

    def per_head(head, carried):
        grad_query, grad_key, grad_value = carried
        scores, query_head, key_head = head_scores(queries, key_part, allowed, head)
        value_head = head_slice(value_part, head)
        grad_head = head_slice(grad_mixed, head)
        probs = jnp.exp(scores - lax.dynamic_slice_in_dim(log_total, head, 1, 1))
        grad_probs = dot_back(grad_head, value_head)
        grad_scores = (
            probs * (grad_probs - jnp.sum(probs * grad_probs, axis=1, keepdims=True))
        ).astype(jnp.bfloat16)
        part_query = jnp.dot(grad_scores, key_head, preferred_element_type=jnp.float32) * HEAD ** (
            -0.5
        )
        part_key = transpose_dot(grad_scores, query_head) * HEAD ** (-0.5)
        part_value = transpose_dot(probs.astype(jnp.bfloat16), grad_head)
        grad_query = lax.dynamic_update_slice_in_dim(grad_query, part_query, head * HEAD, 1)
        grad_key = lax.dynamic_update_slice_in_dim(grad_key, part_key, head * HEAD, 1)
        grad_value = lax.dynamic_update_slice_in_dim(grad_value, part_value, head * HEAD, 1)
        return (grad_query, grad_key, grad_value)

    start = (
        jnp.zeros(queries.shape, jnp.float32),
        jnp.zeros(key_part.shape, jnp.float32),
        jnp.zeros(value_part.shape, jnp.float32),
    )
    return lax.fori_loop(0, HEADS, per_head, start)


def on_device(
    block_input,
    cotangent,
    norm_gain,
    norm_bias,
    w_qkv,
    w_out,
    w_query,
    w_keyval,
    w_cross,
    w_up,
    b_up,
    w_down,
    b_down,
    row_page,
    lengths,
):
    inputs = block_input[0].astype(jnp.float32)
    tokens_here, width = inputs.shape
    half = tokens_here // 2
    columns = tokens_here // WIN
    scales = norm_gain[0]
    shifts = norm_bias[0]
    device = lax.axis_index("page")
    is_query = lax.axis_index("stream") == 1
    length = lengths[0]
    positions = jnp.arange(tokens_here)
    ext_index = jnp.arange(2 * tokens_here)
    ext_row = ext_index // columns
    ext_col = ext_index % columns
    own_row = positions // columns + SHIFT
    own_col = positions % columns
    padded_pages = jnp.concatenate([row_page[-SHIFT:], row_page, row_page[:SHIFT]])
    local_pages = lax.dynamic_slice_in_dim(padded_pages, device * WIN, 2 * WIN)
    key_page = jnp.repeat(local_pages, columns)
    query_page = key_page[half : half + tokens_here]
    own_window = (own_col - SHIFT) % columns // WIN
    ext_window = (ext_col - SHIFT) % columns // WIN
    visual_mask = ((own_row // WIN)[:, None] == (ext_row // WIN)[None, :]) & (
        query_page[:, None] == key_page[None, :]
    )
    visual_mask = (
        visual_mask
        & (own_window[:, None] == ext_window[None, :])
        & ((own_col < SHIFT)[:, None] == (ext_col < SHIFT)[None, :])
    )
    key_slot = ext_index - half
    query_mask = (
        (key_slot[None, :] >= 0)
        & (key_slot[None, :] <= positions[:, None])
        & (key_slot[None, :] < length)
    )
    self_mask = jnp.where(is_query, query_mask, visual_mask)
    cross_mask = ((positions < length) | is_query)[None, :]
    first, unit_one, inverse_one = layer_norm(inputs, scales[:, 0], shifts[:, 0])
    first = first.astype(jnp.bfloat16)
    packed = jnp.dot(first, w_qkv[0], preferred_element_type=jnp.float32).astype(jnp.bfloat16)
    queries = packed[:, :width]
    key_value = packed[:, width:]
    extended = extended_2(key_value, (("page", 0),), half)
    self_mixed, self_log = attend_forward(
        queries, extended[:, :width], extended[:, width:], self_mask
    )
    self_mixed = self_mixed.astype(jnp.bfloat16)
    after_self = inputs + jnp.dot(self_mixed, w_out[0], preferred_element_type=jnp.float32)
    second, unit_two, inverse_two = layer_norm(after_self, scales[:, 1], shifts[:, 1])
    second = second.astype(jnp.bfloat16)
    partner = from_partner(second, "stream", 0)
    cross_queries = jnp.dot(second, w_query[0], preferred_element_type=jnp.float32).astype(
        jnp.bfloat16
    )
    cross_pair = jnp.dot(partner, w_keyval[0], preferred_element_type=jnp.float32).astype(
        jnp.bfloat16
    )
    cross_mixed, cross_log = attend_forward(
        cross_queries, cross_pair[:, :width], cross_pair[:, width:], cross_mask
    )
    cross_mixed = cross_mixed.astype(jnp.bfloat16)
    after_cross = after_self + jnp.dot(cross_mixed, w_cross[0], preferred_element_type=jnp.float32)
    third, unit_three, inverse_three = layer_norm(after_cross, scales[:, 2], shifts[:, 2])
    third = third.astype(jnp.bfloat16)
    pre_act = jnp.dot(third, w_up[0], preferred_element_type=jnp.float32) + b_up[0]
    gelu_tanh = partial(jax.nn.gelu, approximate=True)
    gate_act, gelu_back = jax.vjp(gelu_tanh, pre_act)
    hidden = gate_act.astype(jnp.bfloat16)
    output = (
        after_cross + jnp.dot(hidden, w_down[0], preferred_element_type=jnp.float32) + b_down[0]
    )
    upstream = cotangent[0].astype(jnp.float32)
    up_low = upstream.astype(jnp.bfloat16)
    grad_down_bias = jnp.sum(up_low.astype(jnp.float32), axis=0)
    grad_down = transpose_dot(hidden, up_low)
    grad_pre = gelu_back(dot_back(up_low, w_down[0]))[0]
    pre_low = grad_pre.astype(jnp.bfloat16)
    grad_up_bias = jnp.sum(pre_low.astype(jnp.float32), axis=0)
    grad_up = transpose_dot(third, pre_low)
    back_three, gain_three, shift_three = norm_back(
        dot_back(pre_low, w_up[0]), unit_three, inverse_three, scales[:, 2]
    )
    grad_cross_in = upstream + back_three
    cross_low = grad_cross_in.astype(jnp.bfloat16)
    grad_cross = transpose_dot(cross_mixed, cross_low)
    grad_cmix = dot_back(cross_low, w_cross[0]).astype(jnp.bfloat16)
    cross_dq, cross_dk, cross_dv = attend_backward(
        cross_queries,
        cross_pair[:, :width],
        cross_pair[:, width:],
        cross_mask,
        cross_log,
        grad_cmix,
    )
    query_low = cross_dq.astype(jnp.bfloat16)
    pair_low = jnp.concatenate([cross_dk, cross_dv], 1).astype(jnp.bfloat16)
    grad_query = transpose_dot(second, query_low)
    grad_keyval = transpose_dot(partner, pair_low)
    returned = from_partner(dot_back(pair_low, w_keyval[0]).astype(jnp.bfloat16), "stream", 0)
    second_grad = dot_back(query_low, w_query[0]) + returned.astype(jnp.float32)
    back_two, gain_two, shift_two = norm_back(second_grad, unit_two, inverse_two, scales[:, 1])
    grad_self_in = grad_cross_in + back_two
    self_low = grad_self_in.astype(jnp.bfloat16)
    grad_out = transpose_dot(self_mixed, self_low)
    grad_smix = dot_back(self_low, w_out[0]).astype(jnp.bfloat16)
    self_dq, self_dk, self_dv = attend_backward(
        queries, extended[:, :width], extended[:, width:], self_mask, self_log, grad_smix
    )
    ext_grads = jnp.concatenate([self_dk, self_dv], 1)
    rims = jnp.concatenate([ext_grads[:half], ext_grads[half + tokens_here :]], 0)
    arrived = extended_2(rims.astype(jnp.bfloat16), (("page", 0),), half).astype(rims.dtype)
    own_grads = ext_grads[half : half + tokens_here] + jnp.concatenate(
        [arrived[:half], arrived[half + tokens_here :]], 0
    )
    packed_grad = jnp.concatenate([self_dq, own_grads], 1).astype(jnp.bfloat16)
    grad_qkv = transpose_dot(first, packed_grad)
    back_one, gain_one, shift_one = norm_back(
        dot_back(packed_grad, w_qkv[0]), unit_one, inverse_one, scales[:, 0]
    )
    input_grad = (grad_self_in + back_one).astype(jnp.bfloat16)
    grad_gain = jnp.stack([gain_one, gain_two, gain_three], 1)
    grad_shift = jnp.stack([shift_one, shift_two, shift_three], 1)
    summed = (
        lax.psum_scatter(grad_gain, "page", scatter_dimension=0, tiled=True),
        lax.psum_scatter(grad_shift, "page", scatter_dimension=0, tiled=True),
        lax.psum_scatter(grad_qkv, "page", scatter_dimension=0, tiled=True),
        lax.psum_scatter(grad_out, "page", scatter_dimension=0, tiled=True),
        lax.psum_scatter(grad_query, "page", scatter_dimension=0, tiled=True),
        lax.psum_scatter(grad_keyval, "page", scatter_dimension=0, tiled=True),
        lax.psum_scatter(grad_cross, "page", scatter_dimension=0, tiled=True),
        lax.psum_scatter(grad_up, "page", scatter_dimension=0, tiled=True),
        lax.psum_scatter(grad_up_bias, "page", scatter_dimension=0, tiled=True),
        lax.psum_scatter(grad_down, "page", scatter_dimension=0, tiled=True),
        lax.psum_scatter(grad_down_bias, "page", scatter_dimension=0, tiled=True),
    )
    return (
        output.astype(jnp.bfloat16)[None],
        input_grad[None],
        summed[0][None],
        summed[1][None],
        summed[2][None],
        summed[3][None],
        summed[4][None],
        summed[5][None],
        summed[6][None],
        summed[7][None],
        summed[8][None],
        summed[9][None],
        summed[10][None],
    )


def solution(mesh):
    placed = (
        P("stream", "page", None),
        P("stream", "page", None),
        P("stream", None, None),
        P("stream", None, None),
        P("stream", None, None),
        P("stream", None, None),
        P("stream", None, None),
        P("stream", None, None),
        P("stream", None, None),
        P("stream", None, None),
        P("stream", None),
        P("stream", None, None),
        P("stream", None),
        P(),
        P("page"),
    )
    return jax.shard_map(
        on_device,
        mesh=mesh,
        in_specs=placed,
        out_specs=(
            P("stream", "page", None),
            P("stream", "page", None),
            P("stream", "page", None),
            P("stream", "page", None),
            P("stream", "page", None),
            P("stream", "page", None),
            P("stream", "page", None),
            P("stream", "page", None),
            P("stream", "page", None),
            P("stream", "page", None),
            P("stream", "page"),
            P("stream", "page", None),
            P("stream", "page"),
        ),
        check_vma=False,
    )
```

profile of v0, /device:TPU:0, one launch (start us, length us, event | category | flops | bytes accessed | tf_op | source)
XLA Modules:
  0.0 1389.7 jit_solution(16017729610921970115)
XLA Ops:
  17.1 5.1 collective-permute-start.1
  39.0 115.0 %while.68 = (s32[]{:T(128)}, bf16[576,768]{0,1:T(8,128)(2,1)}, f32[576,12]{0,1:T(8,128)}, bf16[576,768]{1,0:T(8,128)(2,1)}, bf16[1152,768]{1,0:T(8,128)(2,1)}, /...) while((s32[]{:T(128)}, bf16[576,768]{0,1:T(8,128)(2,1)}, ...), condition=%wide.region_5.6_spmd.clone, body=%wide.region_2.5_spmd.clone.sunk | while | flops 182476224 | bytes 19579980 | solution.py:102
  45.4 3.2 fusion.257
  55.0 3.2 fusion.257
  58.2 2.9 fusion.255
  64.6 3.2 fusion.257
  74.1 3.2 fusion.257
  83.7 3.2 fusion.257
  86.9 2.9 fusion.255
  93.3 3.2 fusion.257
  96.5 2.9 fusion.255
  102.9 3.2 fusion.257
  112.5 3.2 fusion.257
  122.1 3.2 fusion.257
  131.7 3.2 fusion.257
  134.9 2.9 fusion.255
  141.2 3.2 fusion.257
  150.8 3.2 fusion.257
  161.3 3.5 convolution_convert_fusion.4
  164.8 9.4 collective-permute-done.2
  179.8 88.3 %while.69 = (s32[]{:T(128)}, bf16[576,768]{0,1:T(8,128)(2,1)}, f32[576,12]{0,1:T(8,128)}, bf16[576,768]{1,0:T(8,128)(2,1)}, bf16[576,768]{1,0:T(8,128)(2,1)}, /*...) while((s32[]{:T(128)}, bf16[576,768]{0,1:T(8,128)(2,1)}, ...), condition=%wide.region_11.12_spmd.clone, body=%wide.region_8.11_spmd.clone.sunk | while | flops 87589440 | bytes 10074440 | solution.py:102
  268.1 3.2 fusion.207
  272.0 5.1 fusion.79
  277.1 11.8 convert_reduce_fusion
  288.9 3.8 multiply_reduce_fusion.2
  299.1 126.4 %while.70 = (s32[]{:T(128)}, bf16[576,768]{0,1:T(8,128)(2,1)}, bf16[576,768]{0,1:T(8,128)(2,1)}, bf16[576,768]{0,1:T(8,128)(2,1)}, bf16[576,768]{1,0:T(8,128)(2,...) while((s32[]{:T(128)}, bf16[576,768]{0,1:T(8,128)(2,1)}, ...), condition=%wide.region_18.19_spmd.clone, body=%wide.region_16.18_spmd.clone.sunk | while | flops 215396928 | bytes 11494980 | solution.py:132
  425.6 5.1 fusion.116
  433.2 14.1 %collective-permute-done.3 = bf16[576,768]{1,0:T(8,128)(2,1)} collective-permute-done((bf16[576,768]{1,0:T(8,128)(2,1)}, bf16[576,768]{1,0:T(8,128)(2,1)}, u32[]{:S(2)}, u32[]{:S(2)}) %collective-permute-start.3) | collective-permute-done | bytes 884768 | tf_op jit(solution)/shard_map/ppermute | solution.py:38
  447.3 4.7 multiply_reduce_fusion.3
  460.2 147.7 %while.71 = (s32[]{:T(128)}, bf16[576,768]{0,1:T(8,128)(2,1)}, f32[1152,768]{0,1:T(8,128)}, f32[1152,768]{0,1:T(8,128)}, bf16[576,768]{1,0:T(8,128)(2,1)}, /*ind...) while((s32[]{:T(128)}, bf16[576,768]{0,1:T(8,128)(2,1)}, ...), condition=%wide.region_23.24_spmd.clone, body=%wide.region_21.23_spmd.clone.sunk | while | flops 438054336 | bytes 22211884 | solution.py:132
  462.6 3.3 multiply_reduce_fusion.14
  474.9 3.3 multiply_reduce_fusion.14
  487.2 3.3 multiply_reduce_fusion.14
  499.5 3.3 multiply_reduce_fusion.14
  511.8 3.3 multiply_reduce_fusion.14
  524.1 3.3 multiply_reduce_fusion.14
  536.4 3.3 multiply_reduce_fusion.14
  548.7 3.3 multiply_reduce_fusion.14
  561.1 3.3 multiply_reduce_fusion.14
  573.4 3.3 multiply_reduce_fusion.14
  585.7 3.3 multiply_reduce_fusion.14
  598.0 3.3 multiply_reduce_fusion.14
  607.9 5.2 copy.29
  613.1 5.2 copy.30
  618.3 3.5 fusion.65
  623.1 6.6 collective-permute-start.4
  635.2 3.6 collective-permute-done.4
  645.6 4.4 fusion.105
  656.1 4.0 fusion.208
  660.2 4.3 fusion.151
  664.6 4.3 fusion.154
  669.0 6.0 fusion.122
  675.1 8.0 fusion.113
  683.4 10.3 fusion.198
  693.7 12.0 fusion.137
  708.3 68.3 %all-reduce.2 = (f32[3072]{0:T(1024)}, f32[768]{0:T(1024)S(1)}) all-reduce(f32[3072]{0:T(1024)} %get-tuple-element.945, f32[768]{0:T(1024)S(1)} %copy-done.37), channel_id=10, replica_groups=mesh['stream'=2,'page'=16] {'page'}, use_global_device_ids=true, to_apply=%region_41.42.clone | all-reduce | flops 3840 | bytes 30720
  778.6 10.3 fusion.119
  793.3 51.6 %reduce-scatter.18.cloned.1.call-done = f32[48,768]{1,0:T(8,128)} async-done(((f32[768,768]{1,0:T(8,128)}), f32[48,768]{1,0:T(8,128)}) %reduce-scatter.18.cloned.1.call-update) | async-done | bytes 147472 | tf_op jit(solution)/shard_map/reduce_scatter | solution.py:279
  844.9 66.7 %reduce-scatter.22.cloned.1.call-done = f32[48,768]{1,0:T(8,128)} async-done(((f32[768,768]{1,0:T(8,128)}), f32[48,768]{1,0:T(8,128)}) %reduce-scatter.22.cloned.1.call-update) | async-done | bytes 147472 | tf_op jit(solution)/shard_map/reduce_scatter | solution.py:281
  911.6 66.3 %reduce-scatter.16.cloned.1.call-done = f32[48,768]{1,0:T(8,128)} async-done(((f32[768,768]{1,0:T(8,128)}), f32[48,768]{1,0:T(8,128)}) %reduce-scatter.16.cloned.1.call-update) | async-done | bytes 147472 | tf_op jit(solution)/shard_map/reduce_scatter | solution.py:278
  977.9 79.4 %reduce-scatter.20.cloned.1.call-done = f32[48,1536]{1,0:T(8,128)} async-done(((f32[768,1536]{1,0:T(8,128)}), f32[48,1536]{1,0:T(8,128)}) %reduce-scatter.20.cloned.1.call-update) | async-done | bytes 294928 | tf_op jit(solution)/shard_map/reduce_scatter | solution.py:280
  1057.3 93.7 %reduce-scatter.14.cloned.1.call-done = f32[48,2304]{1,0:T(8,128)} async-done(((f32[768,2304]{1,0:T(8,128)}), f32[48,2304]{1,0:T(8,128)}) %reduce-scatter.14.cloned.1.call-update) | async-done | bytes 442384 | tf_op jit(solution)/shard_map/reduce_scatter | solution.py:277
  1151.0 116.1 %reduce-scatter.24.cloned.1.call-done = f32[48,3072]{1,0:T(8,128)} async-done(((f32[768,3072]{1,0:T(8,128)}), f32[48,3072]{1,0:T(8,128)}) %reduce-scatter.24.cloned.1.call-update) | async-done | bytes 589840 | tf_op jit(solution)/shard_map/reduce_scatter | solution.py:282
  1267.1 115.8 %reduce-scatter.26.cloned.1.call-done = f32[192,768]{1,0:T(8,128)} async-done(((f32[3072,768]{1,0:T(8,128)}), f32[192,768]{1,0:T(8,128)}) %reduce-scatter.26.cloned.1.call-update) | async-done | bytes 589840 | tf_op jit(solution)/shard_map/reduce_scatter | solution.py:284
  (640 shorter events, 471.0 us)
Async XLA Ops:
  7.2 5.7 copy-start
  7.2 783.3 %reduce-scatter.30.cloned.1.call-start = ((), (), s32[]{:S(2)}) async-start(), calls=%async_computation.17 | async-start | bytes 417792
  7.2 5.6 copy-start.12
  10.6 4.7 copy-start.21
  12.2 3.1 copy-start.23
  15.3 6.9 copy-start.46
  16.7 16.6 %collective-permute-start = (bf16[288,1536]{1,0:T(8,128)(2,1)}, bf16[288,1536]{1,0:T(8,128)(2,1)}, u32[]{:S(2)}, u32[]{:S(2)}) collective-permute-start(bf16[288,1536]{1,0:T(8,128)(2,1)} %get-tuple-element.930), channel_id=1, source_target_pairs={{0,1},{1,2},{2,3},{3,4},{4,5},{5,6},{6,7},{7,8},{8,9},{9,10},{10,1... | collective-permute-start | bytes 2654216 | tf_op jit(solution)/shard_map/ppermute | solution.py:25
  17.1 16.1 %collective-permute-start.1 = (bf16[288,1536]{1,0:T(8,128)(2,1)}, bf16[288,1536]{1,0:T(8,128)(2,1)}, u32[]{:S(2)}, u32[]{:S(2)}) collective-permute-start(bf16[288,1536]{1,0:T(8,128)(2,1)} %get-tuple-element.931), channel_id=1, source_target_pairs={{1,0},{2,1},{3,2},{4,3},{5,4},{6,5},{7,6},{8,7},{9,8},{10,9},{11,1... | collective-permute-start | bytes 2654216 | tf_op jit(solution)/shard_map/ppermute | solution.py:26
  45.4 3.2 copy-start.41
  55.0 3.2 copy-start.41
  58.2 2.9 copy-start.40
  64.6 3.2 copy-start.41
  74.1 3.2 copy-start.41
  83.7 3.2 copy-start.41
  86.9 2.9 copy-start.40
  93.3 3.2 copy-start.41
  96.5 2.9 copy-start.40
  102.9 3.2 copy-start.41
  112.5 3.2 copy-start.41
  115.7 2.9 copy-start.40
  122.1 3.2 copy-start.41
  125.3 2.9 copy-start.40
  131.7 3.2 copy-start.41
  134.9 2.9 copy-start.40
  141.2 3.2 copy-start.41
  144.4 2.9 copy-start.40
  150.8 3.2 copy-start.41
  159.3 14.8 %collective-permute-start.2 = (bf16[576,768]{1,0:T(8,128)(2,1)}, bf16[576,768]{1,0:T(8,128)(2,1)}, u32[]{:S(2)}, u32[]{:S(2)}) collective-permute-start(bf16[576,768]{1,0:T(8,128)(2,1)} %add_convert_fusion.2), channel_id=1, source_target_pairs={{0,16},{16,0},{1,17},{17,1},{2,18},{18,2},{3,19},{19,3},{4,20},{20... | collective-permute-start | bytes 2654216 | tf_op jit(solution)/shard_map/ppermute | solution.py:38
  161.3 12.8 copy-start.50
  271.2 21.5 %copy-start.5 = (f32[576,768]{1,0:T(8,128)}, f32[576,768]{1,0:T(8,128)S(1)}, u32[]{:S(2)}) copy-start(f32[576,768]{1,0:T(8,128)S(1)} %get-tuple-element.941) | copy-start | bytes 5308420
  272.0 5.2 copy-start.20
  272.0 5.2 copy-start.52
  272.0 16.9 %slice-start = ((s8[4718592]{0:T(1024)(128)(4,1)}), s8[4194304]{0:T(1024)(128)(4,1)S(1)}, s32[]{:S(2)}) async-start(s8[4718592]{0:T(1024)(128)(4,1)} %bitcast.165), calls=%async_computation.18 | async-start | bytes 8388608
  277.1 11.8 copy-start.54
  277.1 11.8 slice-start.1
  288.9 3.9 copy-start.16
  425.6 21.7 %copy-start.32 = (f32[576]{0:T(1024)S(1)}, f32[576]{0:T(1024)}, u32[]{:S(2)}) copy-start(f32[576]{0:T(1024)} %copy-done.31) | copy-start | bytes 6916
  430.7 16.6 %collective-permute-start.3 = (bf16[576,768]{1,0:T(8,128)(2,1)}, bf16[576,768]{1,0:T(8,128)(2,1)}, u32[]{:S(2)}, u32[]{:S(2)}) collective-permute-start(bf16[576,768]{1,0:T(8,128)(2,1)} %fusion.116), channel_id=1, source_target_pairs={{0,16},{16,0},{1,17},{17,1},{2,18},{18,2},{3,19},{19,3},{4,20},{20... | collective-permute-start | bytes 2654216 | tf_op jit(solution)/shard_map/ppermute | solution.py:38
  447.3 4.7 copy-start.7
  447.3 4.7 copy-start.11
  447.3 4.7 copy-start.34
  447.3 4.7 copy-start.36
  621.7 8.0 copy-start.45
  621.7 8.5 copy-start.44
  623.1 15.6 %collective-permute-start.4 = (bf16[288,1536]{1,0:T(8,128)(2,1)}, bf16[288,1536]{1,0:T(8,128)(2,1)}, u32[]{:S(2)}, u32[]{:S(2)}) collective-permute-start(bf16[288,1536]{1,0:T(8,128)(2,1)} %get-tuple-element.926), channel_id=1, source_target_pairs={{0,1},{1,2},{2,3},{3,4},{4,5},{5,6},{6,7},{7,8},{8,9},{9,10},{10,1... | collective-permute-start | bytes 2654216 | tf_op jit(solution)/shard_map/ppermute | solution.py:25
  629.7 10.9 collective-permute-start.5
  640.6 3.6 copy-start.4
  645.6 4.4 copy-start.15
  645.6 4.4 copy-start.39
  652.3 139.6 %reduce-scatter.28.cloned.1.call-start = ((), (), s32[]{:S(2)}) async-start(), calls=%async_computation.16 | async-start | bytes 417792
  656.0 188.9 %reduce-scatter.18.cloned.1.call-start = ((), (), s32[]{:S(2)}) async-start(), calls=%async_computation.11 | async-start | bytes 2506752 | tf_op jit(solution)/shard_map/reduce_scatter | solution.py:279
  660.1 251.5 %reduce-scatter.22.cloned.1.call-start = ((), (), s32[]{:S(2)}) async-start(), calls=%async_computation.13 | async-start | bytes 2506752 | tf_op jit(solution)/shard_map/reduce_scatter | solution.py:281
  664.5 313.4 %reduce-scatter.16.cloned.1.call-start = ((), (), s32[]{:S(2)}) async-start(), calls=%async_computation.10 | async-start | bytes 2506752 | tf_op jit(solution)/shard_map/reduce_scatter | solution.py:278
  668.9 388.4 %reduce-scatter.20.cloned.1.call-start = ((), (), s32[]{:S(2)}) async-start(), calls=%async_computation.12 | async-start | bytes 5013504 | tf_op jit(solution)/shard_map/reduce_scatter | solution.py:280
  675.0 476.0 %reduce-scatter.14.cloned.1.call-start = ((), (), s32[]{:S(2)}) async-start(), calls=%async_computation.9 | async-start | bytes 7520256 | tf_op jit(solution)/shard_map/reduce_scatter | solution.py:277
  683.1 584.0 %reduce-scatter.24.cloned.1.call-start = ((), (), s32[]{:S(2)}) async-start(), calls=%async_computation.14 | async-start | bytes 10027008 | tf_op jit(solution)/shard_map/reduce_scatter | solution.py:282
  693.7 689.2 %reduce-scatter.26.cloned.1.call-start = ((), (), s32[]{:S(2)}) async-start(), calls=%async_computation.15 | async-start | bytes 10027008 | tf_op jit(solution)/shard_map/reduce_scatter | solution.py:284
  778.5 10.4 copy-start.48
  778.5 10.4 copy-start.47
  778.5 10.4 copy-start.9
  778.5 10.4 copy-start.14
  778.5 10.4 copy-start.18
  778.5 10.4 copy-start.25
  778.5 10.4 copy-start.28
  (63 other events, 113.3 us)
Sparse Core Ops, SparseCore 0:
  652.5 67.4 reduce-scatter.29
  723.9 54.5 reduce-scatter.27
  782.8 62.0 reduce-scatter.17
  849.6 62.0 reduce-scatter.21
  915.8 62.0 reduce-scatter.15
  982.7 74.5 reduce-scatter.19
  1061.8 89.1 reduce-scatter.13
  1156.2 110.8 reduce-scatter.23
  1271.8 111.0 reduce-scatter.25
where the time goes:
time: 1400 us; the launch traced here: 1390 us
  waiting for transfers between devices  621 us (44%)
  matrix products  473 us (34%)
  local copies, waits for them, and re-layouts  138 us (10%)
  blocking collectives  68.3 us (5%)
  other arithmetic  54.2 us (4%)
  starting transfers between devices  17.2 us (1%)
  between operations  16.6 us (1%)
    dot_general x79, matrix products, dot_back(): lax.dot_general(left, right, (((1,), (1,)), ((), ())), preferred_element_...  181 us
    dot_general x55, matrix products, transpose_dot(): lax.dot_general(left, right, (((0,), (0,)), ((), ())), preferred_element_...  146 us
    reduce_scatter x1, waiting for transfers between devices, on_device(): lax.psum_scatter(grad_up, 'page', scatter_dimension=0, tiled=True)  116 us
    reduce_scatter x1, waiting for transfers between devices, on_device(): lax.psum_scatter(grad_down, 'page', scatter_dimension=0, tiled=True)  116 us
    reduce_scatter x1, waiting for transfers between devices, on_device(): lax.psum_scatter(grad_qkv, 'page', scatter_dimension=0, tiled=True)  93.7 us
    reduce_scatter x1, waiting for transfers between devices, on_device(): lax.psum_scatter(grad_keyval, 'page', scatter_dimension=0, tiled=True)  79.4 us
    unnamed x1, blocking collectives  68.3 us
    dot_general x24, matrix products, per_head(): jnp.dot(probs, head_slice(value_part, head), preferred_element_type=jnp.f...  67.6 us
  transfers between devices with their start and end apart: 15, of which 12 were waited for; matrix products, arithmetic and copies ran while one was open for 6% of the time, Pallas kernels for 0%

commit v1 on v0

v1 whole, which is shorter than its diff:
```python
import functools

import jax
import jax.numpy as jnp
from jax import lax
from jax.experimental import pallas as pl
from jax.experimental.pallas import tpu as pltpu
from jax.sharding import PartitionSpec as P

HEADS = 12
HEAD = 64
WIN = 12
SHIFT = 6
NORM_EPS = 1e-05
MASKED = -1e30


def dot_nt(a,b):
    return lax.dot_general(a,b,(((1,),(1,)),((),())),preferred_element_type=jnp.float32)
def dot_nn(a,b):
    return lax.dot_general(a,b,(((1,),(0,)),((),())),preferred_element_type=jnp.float32)

def fill_self_bias(info, bias):
    tokens=bias.shape[0]; half=tokens//2
    cols=tokens//12
    def codes(shape,dim):
        t=lax.broadcasted_iota(jnp.int32,shape,dim)
        row=jnp.zeros(shape,jnp.int32)
        page=jnp.full(shape,info[2],jnp.int32)
        for r in range(1,12):
            inside=t>=r*cols
            row=jnp.where(inside,r,row)
            page=jnp.where(inside,info[2+r],page)
        c=t-row*cols
        win=jnp.zeros(shape,jnp.int32)
        for w in range(1,cols//12):
            win=jnp.where((c>=6+12*(w-1))&(c<6+12*w),w,win)
        win=jnp.where(c>=cols-6,cols//12+1,win)
        slot=jnp.where(t<half,t+half,t-half)
        return page*16+win,slot
    ck,sk=codes((tokens,1),0)
    cq,sq=codes((1,tokens),1)
    length=info[1]
    @pl.when(info[0]==1)
    def _():
        ok=(sk<=sq)&(sk<length)
        bias[...]=jnp.where(ok,0.0,MASKED)
    @pl.when(info[0]==0)
    def _():
        bias[...]=jnp.where(ck==cq,0.0,MASKED)

def fill_cross_bias(info,bias):
    tokens=bias.shape[0]
    t=lax.broadcasted_iota(jnp.int32,bias.shape,0)
    bias[...]=jnp.where((t<info[1])|(info[0]==1),0.0,MASKED)

def lane_pick(e,scale):
    lane=lax.broadcasted_iota(jnp.int32,(1,2*HEAD),1)
    return jnp.where((lane>=HEAD)==bool(e),scale,0.0).astype(jnp.bfloat16)

def fwd_kernel(fill,info,q_ref,k_ref,v_ref,o_ref,lse_ref,bias):
    @pl.when(pl.program_id(0)==0)
    def _():
        fill(info,bias)
    q=q_ref[...]; k=k_ref[...]; v=v_ref[...]
    vt=v.T
    outs=[]
    for e in range(2):
        qe=q*lane_pick(e,HEAD**-0.5)
        st=dot_nt(k,qe)+bias[...]
        mx=jnp.max(st,axis=0,keepdims=True)
        p=jnp.exp(st-mx)
        l=jnp.sum(p,axis=0,keepdims=True)
        ot=dot_nn(vt[e*HEAD:(e+1)*HEAD],p.astype(jnp.bfloat16))
        outs.append(ot*(1.0/l))
        lse_ref[0,e:e+1,:]=mx+jnp.log(l)
    o_ref[...]=jnp.concatenate(outs,0).T.astype(jnp.bfloat16)

def attn_fwd(info,q,k,v,qo,ko,vo,fill,name):
    t=q.shape[0]; d=768; pairs=d//128
    spec=lambda off: pl.BlockSpec((t,128),lambda j,info:(0,off+j))
    return pl.pallas_call(
        functools.partial(fwd_kernel,fill),
        grid_spec=pltpu.PrefetchScalarGridSpec(num_scalar_prefetch=1,grid=(pairs,),
            in_specs=[spec(qo),spec(ko),spec(vo)],
            out_specs=[spec(0),pl.BlockSpec((1,2,t),lambda j,info:(j,0,0))],
            scratch_shapes=[pltpu.VMEM((t,t),jnp.float32)]),
        out_shape=[jax.ShapeDtypeStruct((t,d),jnp.bfloat16),jax.ShapeDtypeStruct((pairs,2,t),jnp.float32)],
        compiler_params=pltpu.CompilerParams(vmem_limit_bytes=32*2**20),
        cost_estimate=pl.CostEstimate(flops=4*t*t*d,bytes_accessed=8*t*d,transcendentals=t*t*12),
        name=name,
    )(info,q,k,v)

def bwd_kernel(fill,info,q_ref,k_ref,v_ref,do_ref,lse_ref,dq_ref,dk_ref,dv_ref,bias):
    @pl.when(pl.program_id(0)==0)
    def _():
        fill(info,bias)
    q=q_ref[...]; k=k_ref[...]; v=v_ref[...]; do=do_ref[...]
    kt=k.T
    dqs=[]; dk=None; dv=None
    for e in range(2):
        qe=q*lane_pick(e,HEAD**-0.5)
        doe=do*lane_pick(e,1.0)
        st=dot_nt(k,qe)+bias[...]
        p=jnp.exp(st-lse_ref[0,e:e+1,:])
        pd=p*dot_nt(v,doe)
        delta=jnp.sum(pd,axis=0,keepdims=True)
        ds=(pd-p*delta).astype(jnp.bfloat16)
        pb=p.astype(jnp.bfloat16)
        dve=dot_nn(pb,doe); dke=dot_nn(ds,qe)
        dv=dve if dv is None else dv+dve
        dk=dke if dk is None else dk+dke
        dqs.append(dot_nn(kt[e*HEAD:(e+1)*HEAD],ds)*HEAD**-0.5)
    dq_ref[...]=jnp.concatenate(dqs,0).T.astype(jnp.bfloat16)
    dk_ref[...]=dk.astype(jnp.bfloat16)
    dv_ref[...]=dv.astype(jnp.bfloat16)

def attn_bwd(info,q,k,v,qo,ko,vo,do,lse,fill,name):
    t=q.shape[0]; d=768; pairs=d//128
    spec=lambda off: pl.BlockSpec((t,128),lambda j,info:(0,off+j))
    sh=jax.ShapeDtypeStruct((t,d),jnp.bfloat16)
    return pl.pallas_call(
        functools.partial(bwd_kernel,fill),
        grid_spec=pltpu.PrefetchScalarGridSpec(num_scalar_prefetch=1,grid=(pairs,),
            in_specs=[spec(qo),spec(ko),spec(vo),spec(0),pl.BlockSpec((1,2,t),lambda j,info:(j,0,0))],
            out_specs=[spec(0)]*3,
            scratch_shapes=[pltpu.VMEM((t,t),jnp.float32)]),
        out_shape=[sh]*3,
        compiler_params=pltpu.CompilerParams(vmem_limit_bytes=32*2**20),
        cost_estimate=pl.CostEstimate(flops=10*t*t*d,bytes_accessed=16*t*d,transcendentals=t*t*12),
        name=name,
    )(info,q,k,v,do,lse)


def narrow_kernel(order, x_ref, dy_ref, *rest):
    send_ref, keep_ref, across, sorted_rows = rest[-4:]
    rows = x_ref.shape[1] // 16
    half = 8 * rows

    @pl.when(pl.program_id(0) == 0)
    def _():
        across[...] = x_ref[...].T
        for i in range(16):
            start = pl.multiple_of(order[i] * rows, 16)
            sorted_rows[i * rows : (i + 1) * rows, :] = across[pl.ds(start, rows), :]

    grad = dot_nn(sorted_rows[...], dy_ref[...]).astype(jnp.bfloat16)
    send_ref[...] = grad[:half].reshape(send_ref.shape)
    keep_ref[...] = grad[half:].reshape(keep_ref.shape)


def grad_narrow(order, x, dy, height, place, carried, name):
    tokens, wide = dy.shape
    steps = wide // 768
    rows = x.shape[1] // 16
    out = jax.ShapeDtypeStruct((8, height, 768), jnp.bfloat16)
    piece = pl.BlockSpec((8, rows, 768), lambda j, order: (0, place + j, 0))
    in_specs = [
        pl.BlockSpec(x.shape, lambda j, order: (0, 0)),
        pl.BlockSpec((tokens, 768), lambda j, order: (0, j)),
    ]
    operands = [order, x, dy]
    aliases = {}
    if carried is not None:
        in_specs += [pl.BlockSpec(memory_space=pl.ANY)] * 2
        operands += list(carried)
        aliases = {3: 0, 4: 1}
    return pl.pallas_call(
        narrow_kernel,
        grid_spec=pltpu.PrefetchScalarGridSpec(
            num_scalar_prefetch=1,
            grid=(steps,),
            in_specs=in_specs,
            out_specs=[piece, piece],
            scratch_shapes=[
                pltpu.VMEM((x.shape[1], tokens), jnp.bfloat16),
                pltpu.VMEM((x.shape[1], tokens), jnp.bfloat16),
            ],
        ),
        out_shape=[out, out],
        input_output_aliases=aliases,
        compiler_params=pltpu.CompilerParams(vmem_limit_bytes=24 * 2**20),
        cost_estimate=pl.CostEstimate(
            flops=2 * tokens * wide * x.shape[1],
            bytes_accessed=2 * (x.size + dy.size + 768 * wide),
            transcendentals=0,
        ),
        name=name,
    )(*operands)


def early_kernel(x_ref, dy_ref, *rest):
    out_ref, across = rest[-2:]

    @pl.when(pl.program_id(0) == 0)
    def _():
        across[...] = x_ref[...].T

    out_ref[...] = dot_nn(across[...], dy_ref[...]).astype(jnp.bfloat16).reshape(out_ref.shape)


def early_down_kernel(x_ref, dy_ref, out_ref):
    out_ref[...] = dot_nn(x_ref[...].T, dy_ref[...]).astype(jnp.bfloat16).reshape(out_ref.shape)


def early_grads(hidden, dy, third, pre_low):
    tokens, deep = hidden.shape
    out = jax.ShapeDtypeStruct((16, 384, 768), jnp.bfloat16)
    cost = pl.CostEstimate(
        flops=2 * tokens * deep * 768, bytes_accessed=2 * 768 * (deep + tokens), transcendentals=0
    )
    params = pltpu.CompilerParams(vmem_limit_bytes=24 * 2**20)
    down = pl.pallas_call(
        early_down_kernel,
        grid=(8,),
        in_specs=[
            pl.BlockSpec((tokens, 384), lambda j: (0, j)),
            pl.BlockSpec(dy.shape, lambda j: (0, 0)),
        ],
        out_specs=pl.BlockSpec((2, 192, 768), lambda j: (j, 0, 0)),
        out_shape=out,
        compiler_params=params,
        cost_estimate=cost,
        name="gdown",
    )(hidden, dy)
    return pl.pallas_call(
        early_kernel,
        grid=(4,),
        in_specs=[
            pl.BlockSpec(third.shape, lambda j: (0, 0)),
            pl.BlockSpec((tokens, 768), lambda j: (0, j)),
            pl.BlockSpec(memory_space=pl.ANY),
        ],
        out_specs=pl.BlockSpec((16, 48, 768), lambda j: (0, 4 + j, 0)),
        out_shape=out,
        scratch_shapes=[pltpu.VMEM((768, tokens), jnp.bfloat16)],
        input_output_aliases={2: 0},
        compiler_params=params,
        cost_estimate=cost,
        name="gup",
    )(third, pre_low, down)


def swap(x, bit):
    return lax.ppermute(x, "page", [(i, i ^ bit) for i in range(16)])


def halved_small(x):
    device = lax.axis_index("page")
    bit = 1
    while x.shape[0] > 1:
        pairs = x.reshape(x.shape[0] // 2, 2, x.shape[1])
        mine = device // bit % 2
        other = lax.dynamic_index_in_dim(pairs, 1 - mine, 1, keepdims=False)
        x = lax.dynamic_index_in_dim(pairs, mine, 1, keepdims=False) + swap(other, bit)
        bit *= 2
    return x[0]


def halved_first(send, keep):
    arrived = swap(send, 1)
    return keep[:4] + arrived[:4], keep[4:] + arrived[4:]


def halved_rest(outgoing, stay):
    for bit, count in ((2, 2), (4, 1), (8, 0)):
        arrived = swap(outgoing, bit)
        if count == 0:
            return stay[0].astype(jnp.float32) + arrived[0].astype(jnp.float32)
        outgoing = stay[:count] + arrived[:count]
        stay = stay[count:] + arrived[count:]


def layer_norm(inputs, scales, shifts):
    average = jnp.mean(inputs, axis=1, keepdims=True)
    centred = inputs - average
    spread = jnp.mean(centred * centred, axis=1, keepdims=True)
    inverse = lax.rsqrt(spread + NORM_EPS)
    unit = centred * inverse
    return (unit * scales + shifts).astype(jnp.bfloat16), unit, inverse


def norm_back(upstream, unit, inverse, scales):
    scaled = upstream * scales
    inner = (
        scaled
        - jnp.mean(scaled, axis=1, keepdims=True)
        - unit * jnp.mean(scaled * unit, axis=1, keepdims=True)
    )
    return (inverse * inner, jnp.sum(upstream * unit, axis=0), jnp.sum(upstream, axis=0))


def matmul(left, right):
    return jnp.dot(left, right, preferred_element_type=jnp.float32)


def gelu_pair(pre):
    root = 0.7978845608028654
    square = pre * pre
    turned = jnp.tanh(root * pre * (1.0 + 0.044715 * square))
    value = 0.5 * pre * (1.0 + turned)
    slope = 0.5 * (1.0 + turned) + 0.5 * pre * (1.0 - turned * turned) * root * (
        1.0 + 3 * 0.044715 * square
    )
    return value, slope


def on_device(
    block_input,
    cotangent,
    norm_gain,
    norm_bias,
    w_qkv,
    w_out,
    w_query,
    w_keyval,
    w_cross,
    w_up,
    b_up,
    w_down,
    b_down,
    row_page,
    lengths,
):
    x = block_input[0]
    dy = cotangent[0]
    tokens, width = x.shape
    half = tokens // 2
    pages = lax.axis_size("page")
    device = lax.axis_index("page")
    stream = lax.axis_index("stream")
    scales = norm_gain[0].T
    shifts = norm_bias[0].T
    padded = jnp.concatenate([row_page, row_page[:SHIFT]])
    info = jnp.concatenate(
        [
            stream.astype(jnp.int32)[None],
            lengths,
            lax.dynamic_slice_in_dim(padded, device * WIN + SHIFT, WIN),
        ]
    )
    stay = [(pages + i, pages + i) for i in range(pages)]
    both = ("stream", "page")
    forth = [((i + 1) % pages, i) for i in range(pages)] + stay
    back = [(i, (i + 1) % pages) for i in range(pages)] + stay

    def to_windows(rows):
        return jnp.concatenate([rows[half:], lax.ppermute(rows[:half], both, forth)])

    def to_bands(rows):
        return jnp.concatenate([lax.ppermute(rows[half:], both, back), rows[:half]])

    def partner_of(rows):
        return lax.ppermute(rows, "stream", [(0, 1), (1, 0)])

    moved = to_windows(x)
    first, unit_one, inverse_one = layer_norm(moved.astype(jnp.float32), scales[0], shifts[0])
    packed = matmul(first, w_qkv[0]).astype(jnp.bfloat16)
    moved_mixed, self_log = attn_fwd(info, packed, packed, packed, 0, 6, 12, fill_self_bias, "selff")
    self_mixed = to_bands(moved_mixed)
    after_self = x.astype(jnp.float32) + matmul(self_mixed, w_out[0])
    second, unit_two, inverse_two = layer_norm(after_self, scales[1], shifts[1])
    partner = partner_of(second)
    cross_q = matmul(second, w_query[0]).astype(jnp.bfloat16)
    cross_pair = matmul(partner, w_keyval[0]).astype(jnp.bfloat16)
    cross_mixed, cross_log = attn_fwd(
        info, cross_q, cross_pair, cross_pair, 0, 0, 6, fill_cross_bias, "crossf"
    )
    after_cross = after_self + matmul(cross_mixed, w_cross[0])
    third, unit_three, inverse_three = layer_norm(after_cross, scales[2], shifts[2])
    pre_act = matmul(third, w_up[0]) + b_up[0]
    value, slope = gelu_pair(pre_act)
    hidden = value.astype(jnp.bfloat16)
    output = after_cross + matmul(hidden, w_down[0]) + b_down[0]
    upstream = dy.astype(jnp.float32)
    grad_down_bias = jnp.sum(upstream, axis=0)
    grad_pre = dot_nt(dy, w_down[0]) * slope
    pre_low = grad_pre.astype(jnp.bfloat16)
    grad_up_bias = jnp.sum(pre_low.astype(jnp.float32), axis=0)
    back_three, gain_three, shift_three = norm_back(
        dot_nt(pre_low, w_up[0]), unit_three, inverse_three, scales[2]
    )
    grad_cross_in = upstream + back_three
    cross_low = grad_cross_in.astype(jnp.bfloat16)
    grad_cmix = dot_nt(cross_low, w_cross[0]).astype(jnp.bfloat16)
    if pages == 16:
        early = early_grads(hidden, dy, third, pre_low)
        grad_cmix, early = lax.optimization_barrier((grad_cmix, early))
        early = lax.psum_scatter(early, "page", scatter_dimension=0, tiled=True)[0]
        ordinal = jnp.arange(16, dtype=jnp.int32)
        turned = 15 - ordinal
        turned = (turned & 1) << 3 | (turned & 2) << 1 | (turned & 4) >> 1 | (turned & 8) >> 3
        order = device.astype(jnp.int32) ^ turned
    cross_dq, cross_dk, cross_dv = attn_bwd(
        info, cross_q, cross_pair, cross_pair, 0, 0, 6, grad_cmix, cross_log,
        fill_cross_bias, "crossb",
    )
    given = dot_nt(cross_dk, w_keyval[0][:, :width]) + dot_nt(cross_dv, w_keyval[0][:, width:])
    returned = partner_of(given.astype(jnp.bfloat16))
    second_grad = dot_nt(cross_dq, w_query[0]) + returned.astype(jnp.float32)
    back_two, gain_two, shift_two = norm_back(second_grad, unit_two, inverse_two, scales[1])
    grad_self_in = grad_cross_in + back_two
    moved_low = to_windows(grad_self_in.astype(jnp.bfloat16))
    grad_smix = dot_nt(moved_low, w_out[0]).astype(jnp.bfloat16)
    if pages == 16:
        part = grad_narrow(order, cross_mixed, cross_low, 192, 0, None, "gcross")
        part = grad_narrow(order, second, cross_dq, 192, 1, part, "gquery")
        part = grad_narrow(order, partner, cross_dk, 192, 2, part, "gkey")
        part = grad_narrow(order, partner, cross_dv, 192, 3, part, "gvalue")
        cross_part = halved_first(*part)
        grad_smix, cross_part = lax.optimization_barrier((grad_smix, cross_part))
        cross_part = halved_rest(*cross_part)
    self_dq, self_dk, self_dv = attn_bwd(
        info, packed, packed, packed, 0, 6, 12, grad_smix, self_log, fill_self_bias, "selfb",
    )
    grad_first = (
        dot_nt(self_dq, w_qkv[0][:, :width])
        + dot_nt(self_dk, w_qkv[0][:, width : 2 * width])
        + dot_nt(self_dv, w_qkv[0][:, 2 * width :])
    )
    back_one, gain_one, shift_one = norm_back(grad_first, unit_one, inverse_one, scales[0])
    input_grad = to_bands((moved_low.astype(jnp.float32) + back_one).astype(jnp.bfloat16))
    small = [gain_one, gain_two, gain_three, shift_one, shift_two, shift_three, grad_down_bias]
    if pages == 16:
        part = grad_narrow(order, moved_mixed, moved_low, 192, 0, None, "gout")
        part = grad_narrow(order, first, self_dq, 192, 1, part, "gq")
        part = grad_narrow(order, first, self_dk, 192, 2, part, "gk")
        part = grad_narrow(order, first, self_dv, 192, 3, part, "gv")
        self_part = halved_rest(*halved_first(*part))

        def across(block, first_row, count):
            return jnp.concatenate(
                [block[first_row + 48 * i : first_row + 48 * (i + 1)] for i in range(count)], 1
            )

        early = early.astype(jnp.float32)
        grad_down = early[:192]
        grad_up = across(early, 192, 4)
        grad_cross = across(cross_part, 0, 1)
        grad_query = across(cross_part, 48, 1)
        grad_keyval = across(cross_part, 96, 2)
        grad_out = across(self_part, 0, 1)
        grad_qkv = across(self_part, 48, 3)
    else:

        def scattered(left, right):
            grad = lax.dot_general(
                left, right, (((0,), (0,)), ((), ())), preferred_element_type=jnp.float32
            )
            return lax.psum_scatter(grad, "page", scatter_dimension=0, tiled=True)

        grad_down = scattered(hidden, dy)
        grad_up = scattered(third, pre_low)
        grad_cross = scattered(cross_mixed, cross_low)
        grad_query = scattered(second, cross_dq)
        grad_keyval = scattered(partner, jnp.concatenate([cross_dk, cross_dv], 1))
        grad_out = scattered(moved_mixed, moved_low)
        grad_qkv = scattered(first, jnp.concatenate([self_dq, self_dk, self_dv], 1))
    stacked = jnp.concatenate(
        [v.reshape(pages, width // pages) for v in small]
        + [grad_up_bias.reshape(pages, grad_up_bias.shape[0] // pages)],
        1,
    )
    if pages == 16:
        summed = halved_small(stacked)
    else:
        summed = lax.psum_scatter(stacked, "page", scatter_dimension=0, tiled=True)[0]
    share = width // pages
    piece = [summed[i * share : (i + 1) * share] for i in range(7)]
    return (
        output.astype(jnp.bfloat16)[None],
        input_grad[None],
        jnp.stack(piece[:3], 1)[None],
        jnp.stack(piece[3:6], 1)[None],
        grad_qkv[None],
        grad_out[None],
        grad_query[None],
        grad_keyval[None],
        grad_cross[None],
        grad_up[None],
        summed[7 * share :][None],
        grad_down[None],
        piece[6][None],
    )


def solution(mesh):
    tokens = P("stream", "page", None)
    whole = P("stream", None, None)
    placed = (tokens, tokens) + (whole,) * 8 + (P("stream", None), whole, P("stream", None))
    return jax.shard_map(
        on_device,
        mesh=mesh,
        in_specs=placed + (P(), P("page")),
        out_specs=(tokens,) * 10 + (P("stream", "page"), tokens, P("stream", "page")),
        check_vma=False,
    )
```

time: 1400 us -> 354 us (0.25)
  waiting for transfers between devices: 621 us -> 103 us
  matrix products: 473 us -> 43.8 us
  local copies, waits for them, and re-layouts: 138 us -> 35.3 us
  Pallas kernels: 0 us -> 87.5 us
  blocking collectives: 68.3 us -> 0 us
  other arithmetic: 54.2 us -> 23.2 us
  starting transfers between devices: 17.2 us -> 38.6 us
    reduce_scatter x7 -> x1, waiting for transfers between devices: 590 us -> 0.01 us  [on_device(): early = lax.psum_scatter(early, 'page', scatter_dimension=0, tiled=True)[0]]
    dot_general x189 -> x17, matrix products: 473 us -> 43.8 us  [the longest x10 26.9 us: dot_nt(): lax.dot_general(a, b, (((1,), (1,)), ((), ())), preferred_element_type=jn...]
    pallas_call x0 -> x14, Pallas kernels: none -> 87.5 us  [the longest x2 32.5 us: attn_bwd(): pl.pallas_call(functools.partial(bwd_kernel, fill), grid_spec=pltpu.Prefe...]
    ppermute x6 -> x18, waiting for transfers between devices: 30.9 us -> 103 us  [the longest x12 66.8 us: swap(): return lax.ppermute(x, 'page', [(i, i ^ bit) for i in range(16)])]
    unnamed x1 -> x0, blocking collectives: 68.3 us -> none
    while x123 -> x0, local copies, waits for them, and re-layouts: 45.1 us -> none
    dynamic_update_slice x24 -> x0, local copies, waits for them, and re-layouts: 32.6 us -> none  [per_head(): lax.dynamic_update_slice_in_dim(log_total, peak + jnp.log(total), head, 1)]
    ppermute x6 -> x18, starting transfers between devices: 16.6 us -> 38.6 us  [the longest x2 22.4 us: to_windows(): lax.ppermute(rows[:half], both, forth)]
  transfers between devices with their start and end apart: 15 -> 19, of which waited for: 12 -> 12; matrix products, arithmetic and copies ran while one was open for 6% -> 14% of each run, Pallas kernels for 0% -> 16%
where the time goes in v1:
time: 354 us; the launch traced here: 347 us
  waiting for transfers between devices  103 us (29%)
  Pallas kernels  87.5 us (25%)
  matrix products  43.8 us (12%)
  starting transfers between devices  38.6 us (11%)
  local copies, waits for them, and re-layouts  35.3 us (10%)
  other arithmetic  23.2 us (7%)
  between operations  15.9 us (4%)
    ppermute x12, waiting for transfers between devices, swap(): return lax.ppermute(x, 'page', [(i, i ^ bit) for i in range(16)])  66.8 us
    pallas_call x2, Pallas kernels, attn_bwd(): pl.pallas_call(functools.partial(bwd_kernel, fill), grid_spec=pltpu.Prefe...  32.5 us
    dot_general x10, matrix products, dot_nt(): lax.dot_general(a, b, (((1,), (1,)), ((), ())), preferred_element_type=jn...  26.9 us
    ppermute x2, starting transfers between devices, to_windows(): lax.ppermute(rows[:half], both, forth)  22.4 us
    pallas_call x8, Pallas kernels, grad_narrow(): pl.pallas_call(narrow_kernel, grid_spec=pltpu.PrefetchScalarGridSpec(num_...  22.1 us
    pallas_call x2, Pallas kernels, attn_fwd(): pl.pallas_call(functools.partial(fwd_kernel, fill), grid_spec=pltpu.Prefe...  21.2 us
    unnamed x139, local copies, waits for them, and re-layouts  17.2 us
    dot_general x7, matrix products, matmul(): return jnp.dot(left, right, preferred_element_type=jnp.float32)  16.9 us
  transfers between devices with their start and end apart: 19, of which 12 were waited for; matrix products, arithmetic and copies ran while one was open for 14% of the time, Pallas kernels for 16%

profile of v1, /device:TPU:0, one launch (start us, length us, event | category | flops | bytes accessed | tf_op | source)
XLA Modules:
  0.0 347.0 jit_solution(2728664287829433814)
XLA Ops:
  7.3 1.3 slice_bitcast_fusion.1
  8.6 7.3 %collective-permute-start = (bf16[288,768]{1,0:T(8,128)(2,1)S(1)}, bf16[288,768]{1,0:T(8,128)(2,1)S(1)}, u32[]{:S(2)}, u32[]{:S(2)}) collective-permute-start(bf16[288,768]{1,0:T(8,128)(2,1)S(1)} %get-tuple-element.167), channel_id=1, source_target_pairs={{1,0},{2,1},{3,2},{4,3},{5,4},{6,5},{7,6},{8,7},{9,8},{10,9},{11,1... | collective-permute-start | bytes 1327112 | tf_op jit(solution)/shard_map/ppermute | solution.py:348
  16.9 4.8 %collective-permute-done = bf16[288,768]{1,0:T(8,128)(2,1)S(1)} collective-permute-done((bf16[288,768]{1,0:T(8,128)(2,1)S(1)}, bf16[288,768]{1,0:T(8,128)(2,1)S(1)}, u32[]{:S(2)}, u32[]{:S(2)}) %collective-permute-start) | collective-permute-done | bytes 442400 | tf_op jit(solution)/shard_map/ppermute | solution.py:348
  22.8 1.1 copy-done.53
  23.9 2.2 convolution_convert_fusion.q_ref.k_ref.v_ref
  26.1 0.9 copy-done.6
  27.1 10.6 %selff.1 = (bf16[576,768]{1,0:T(8,128)(2,1)S(1)}, f32[6,2,576]{2,1,0:T(2,128)S(1)}) custom-call(s32[14]{0:T(128)S(1)} %pad_add_fusion.1.info, bf16[576,2304]{1,0:T(8,128)(2,1)S(1)} %convolution_convert_fusion.q_ref.k_ref.v_ref, bf16[576,2304]{1,0:T(8,128)(2,1)S(1)} %convolution_convert_fusion.q_ref.k_ref.v_ref, ...), custom_call_target="tpu_custom_call" | custom-call | flops 1019215872 | bytes 3538944 | tf_op jit(solution)/shard_map/selff/pallas_call | solution.py:82
  37.7 2.1 collective-permute-start.1
  39.8 10.6 %collective-permute-done.1 = bf16[288,768]{1,0:T(8,128)(2,1)S(1)} collective-permute-done((bf16[288,768]{1,0:T(8,128)(2,1)S(1)}, bf16[288,768]{1,0:T(8,128)(2,1)S(1)}, u32[]{:S(2)}, u32[]{:S(2)}) %collective-permute-start.1) | collective-permute-done | bytes 442400 | tf_op jit(solution)/shard_map/ppermute | solution.py:351
  50.4 1.0 fusion.58
  53.1 13.1 %collective-permute-done.2.x_ref = bf16[576,768]{1,0:T(8,128)(2,1)S(1)} collective-permute-done((bf16[576,768]{1,0:T(8,128)(2,1)S(1)}, bf16[576,768]{1,0:T(8,128)(2,1)S(1)}, u32[]{:S(2)}, u32[]{:S(2)}) %collective-permute-start.2) | collective-permute-done | bytes 884768 | tf_op jit(solution)/shard_map/ppermute | solution.py:354
  66.2 1.5 convolution_convert_fusion.1.k_ref.v_ref
  67.8 10.6 %crossf.1 = (bf16[576,768]{1,0:T(8,128)(2,1)S(1)}, f32[6,2,576]{2,1,0:T(2,128)S(1)}) custom-call(s32[14]{0:T(128)S(1)} %pad_add_fusion.1.info, bf16[576,768]{1,0:T(8,128)(2,1)S(1)} %convolution_convert_fusion.4.q_ref, bf16[576,1536]{1,0:T(8,128)(2,1)S(1)} %convolution_convert_fusion.1.k_ref.v_ref, bf16[576,1536]{1,0:T(8,128)(2,1)S(1)} %convolution_convert_fusion.1.k_ref.v_ref), custom_call_target="tpu_custom_call" | custom-call | flops 1019215872 | bytes 3538944 | tf_op jit(solution)/shard_map/crossf/pallas_call | solution.py:82
  78.5 1.0 fusion.59
  80.6 6.5 %multiply_convert_fusion.1 = (bf16[576,3072]{1,0:T(8,128)(2,1)S(1)}, f32[576,3072]{1,0:T(8,128)}) fusion(f32[3072]{0:T(1024)S(1)} %bitcast.166, bf16[576,768]{1,0:T(8,128)(2,1)S(1)} %add_convert_fusion.3.x_ref, bf16[1,768,3072]{2,1,0:T(8,128)(2,1)S(1)} %bitcast.156), kind=kOutput, calls=%fused_computation.2 | convolution fusion | flops 2735603712 | bytes 16232448 | tf_op jit(solution)/shard_map/dot_general | solution.py:294
  87.1 9.8 %convert_reduce_fusion = (f32[3072]{0:T(1024)S(1)}, bf16[576,3072]{1,0:T(8,128)(2,1)S(1)}) fusion(f32[576,3072]{1,0:T(8,128)} %get-tuple-element.194, f32[3072]{0:T(1024)S(1)} %bitcast.167, bf16[1,3072,768]{2,1,0:T(8,128)(2,1)S(1)} %bitcast.158, bf16[1,576,768]{2,1,0:T(8,128)(2,1)S(1)} %copy-done.10), kind=kOutput, calls=%fused_computation | convolution fusion | flops 2755064832 | bytes 16244736 | tf_op jit(solution)/shard_map/dot_general | solution.py:19
  96.9 3.4 multiply_reduce_fusion
  100.3 2.0 fusion.51
  102.4 1.8 convolution_convert_fusion.3.do_ref
  104.2 6.5 %gdown.1.rest_0_ = bf16[16,384,768]{2,1,0:T(8,128)(2,1)S(1)} custom-call(bf16[576,3072]{1,0:T(8,128)(2,1)S(1)} %get-tuple-element.193.x_ref, bf16[576,768]{1,0:T(8,128)(2,1)S(1)} %bitcast.149), custom_call_target="tpu_custom_call" | custom-call | flops 2717908992 | bytes 5603328 | tf_op jit(solution)/shard_map/gdown/pallas_call | solution.py:213
  110.7 5.2 %gup.1 = bf16[16,384,768]{2,1,0:T(8,128)(2,1)S(1)} custom-call(bf16[576,768]{1,0:T(8,128)(2,1)S(1)} %add_convert_fusion.3.x_ref, bf16[576,3072]{1,0:T(8,128)(2,1)S(1)} %get-tuple-element.199.dy_ref, bf16[16,384,768]{2,1,0:T(8,128)(2,1)S(1)} %gdown.1.rest_0_), custom_call_target="tpu_custom_call", output_to_operand_aliasing={{}: (2, {})} | custom-call | flops 2717908992 | bytes 5603328 | tf_op jit(solution)/shard_map/gup/pallas_call | solution.py:226
  115.9 3.6 %copy-done.1 = bf16[16,384,768]{2,1,0:T(8,128)(2,1)} copy-done((bf16[16,384,768]{2,1,0:T(8,128)(2,1)}, bf16[16,384,768]{2,1,0:T(8,128)(2,1)S(1)}, u32[]{:S(2)}) %copy-start.1) | copy-done | bytes 9437208
  119.6 1.2 copy-done.25
  120.8 1.5 copy-done.27
  122.2 1.2 copy-done.29
  123.4 16.2 %crossb.1 = (bf16[576,768]{1,0:T(8,128)(2,1)S(1)}, bf16[576,768]{1,0:T(8,128)(2,1)S(1)}, bf16[576,768]{1,0:T(8,128)(2,1)S(1)}) custom-call(s32[14]{0:T(128)S(1)} %pad_add_fusion.1.info, bf16[576,768]{1,0:T(8,128)(2,1)S(1)} %copy-done.29, bf16[576,1536]{1,0:T(8,128)(2,1)S(1)} %copy-done.27, bf16[576,1536]{1,0:T(8,128)(2,1)S(1)} %copy-done.27, ...), custom_call_target="tpu_custom_call" | custom-call | flops 2548039680 | bytes 7077888 | tf_op jit(solution)/shard_map/crossb/pallas_call | solution.py:122
  141.1 1.8 add_convert_fusion.1
  143.2 1.2 copy-done.14
  144.4 1.2 copy-done.22
  145.6 2.8 gcross.1
  148.4 2.8 gquery.1
  151.2 2.8 gkey.1
  154.0 2.8 gvalue.1
  156.8 3.4 multiply_reduce_fusion.1
  161.0 15.1 %collective-permute-start.4 = (bf16[288,768]{1,0:T(8,128)(2,1)S(1)}, bf16[288,768]{1,0:T(8,128)(2,1)S(1)}, u32[]{:S(2)}, u32[]{:S(2)}) collective-permute-start(bf16[288,768]{1,0:T(8,128)(2,1)S(1)} %get-tuple-element.163), channel_id=1, source_target_pairs={{1,0},{2,1},{3,2},{4,3},{5,4},{6,5},{7,6},{8,7},{9,8},{10,9},{11,1... | collective-permute-start | bytes 1327112 | tf_op jit(solution)/shard_map/ppermute | solution.py:348
  176.1 3.8 %fusion.24 = bf16[1,576,768]{2,1,0:T(8,128)(2,1)} fusion(f32[576,768]{1,0:T(8,128)S(1)} %copy-done.31, bf16[576,3072]{1,0:T(8,128)(2,1)S(1)} %copy-done.9, bf16[1,3072,768]{2,1,0:T(8,128)(2,1)S(1)} %bitcast.160, f32[768]{0:T(1024)S(1)} %reduce.6), kind=kOutput, calls=%fused_computation.55 | convolution fusion | flops 2719236096 | bytes 10914816 | tf_op jit(solution)/shard_map/dot_general | solution.py:294
  184.0 7.3 %collective-permute-done.4 = bf16[288,768]{1,0:T(8,128)(2,1)S(1)} collective-permute-done((bf16[288,768]{1,0:T(8,128)(2,1)S(1)}, bf16[288,768]{1,0:T(8,128)(2,1)S(1)}, u32[]{:S(2)}, u32[]{:S(2)}) %collective-permute-start.4) | collective-permute-done | bytes 442400 | tf_op jit(solution)/shard_map/ppermute | solution.py:348
  192.1 1.3 copy-done.12
  193.4 2.7 gout.1
  197.9 3.6 %slice_add_fusion.2 = (bf16[4,192,768]{2,1,0:T(8,128)(2,1)}, bf16[4,192,768]{2,1,0:T(8,128)(2,1)}) fusion(bf16[8,192,768]{2,1,0:T(8,128)(2,1)} %collective-permute-done.5, bf16[8,192,768]{2,1,0:T(8,128)(2,1)S(1)} %copy-done.3), kind=kLoop, calls=%fused_computation.63 | loop fusion | flops 1179648 | bytes 7077888 | tf_op jit(solution)/shard_map/add | solution.py:262
  201.5 16.3 %selfb.1 = (bf16[576,768]{1,0:T(8,128)(2,1)S(1)}, bf16[576,768]{1,0:T(8,128)(2,1)S(1)}, bf16[576,768]{1,0:T(8,128)(2,1)S(1)}) custom-call(s32[14]{0:T(128)S(1)} %pad_add_fusion.1.info, bf16[576,2304]{1,0:T(8,128)(2,1)S(1)} %copy-done.5, bf16[576,2304]{1,0:T(8,128)(2,1)S(1)} %copy-done.5, bf16[576,2304]{1,0:T(8,128)(2,1)S(1)} %copy-done.5, ...), custom_call_target="tpu_custom_call" | custom-call | flops 2548039680 | bytes 7077888 | tf_op jit(solution)/shard_map/selfb/pallas_call | solution.py:122
  217.8 2.7 gq.1
  220.6 2.7 gk.1
  223.3 2.8 gv.1
  227.0 0.9 fusion.28
  228.2 3.2 fusion.20
  231.3 1.4 concatenate.53
  233.4 1.6 concatenate.61
  237.9 1.3 reshape.166
  240.1 7.3 %collective-permute-start.8 = (f32[4,528]{1,0:T(4,128)S(1)}, f32[4,528]{1,0:T(4,128)S(1)}, u32[]{:S(2)}, u32[]{:S(2)}) collective-permute-start(f32[4,528]{1,0:T(4,128)S(1)} %bitcast.153), channel_id=1, source_target_pairs={{0,2},{1,3},{2,0},{3,1},{4,6},{5,7},{6,4},{7,5},{8,10},{9,11},{10,... | collective-permute-start | bytes 25352 | tf_op jit(solution)/shard_map/ppermute | solution.py:245
  247.4 1.3 broadcast_multiply_fusion.1
  249.7 1.3 reshape.167
  252.3 2.7 fusion.19
  255.9 2.1 slice_add_fusion.1
  257.9 1.8 collective-permute-start.12
  259.7 18.1 %collective-permute-done.15 = bf16[4,192,768]{2,1,0:T(8,128)(2,1)} collective-permute-done((bf16[4,192,768]{2,1,0:T(8,128)(2,1)}, bf16[4,192,768]{2,1,0:T(8,128)(2,1)}, u32[]{:S(2)}, u32[]{:S(2)}) %collective-permute-start.15) | collective-permute-done | bytes 1179680 | tf_op jit(solution)/shard_map/ppermute | solution.py:245
  277.8 1.4 slice_add_fusion.5
  279.9 1.9 collective-permute-start.6
  282.4 10.1 %collective-permute-done.16 = bf16[2,192,768]{2,1,0:T(8,128)(2,1)S(1)} collective-permute-done((bf16[2,192,768]{2,1,0:T(8,128)(2,1)S(1)}, bf16[2,192,768]{2,1,0:T(8,128)(2,1)S(1)}, u32[]{:S(2)}, u32[]{:S(2)}) %collective-permute-start.16) | collective-permute-done | bytes 589856 | tf_op jit(solution)/shard_map/ppermute | solution.py:245
  292.6 14.1 %collective-permute-done.12 = bf16[4,192,768]{2,1,0:T(8,128)(2,1)S(1)} collective-permute-done((bf16[4,192,768]{2,1,0:T(8,128)(2,1)S(1)}, bf16[4,192,768]{2,1,0:T(8,128)(2,1)S(1)}, u32[]{:S(2)}, u32[]{:S(2)}) %collective-permute-start.12) | collective-permute-done | bytes 1179680 | tf_op jit(solution)/shard_map/ppermute | solution.py:245
  309.2 1.0 maximum_bitcast_fusion
  310.2 10.9 %collective-permute-done.13 = bf16[2,192,768]{2,1,0:T(8,128)(2,1)S(1)} collective-permute-done((bf16[2,192,768]{2,1,0:T(8,128)(2,1)S(1)}, bf16[2,192,768]{2,1,0:T(8,128)(2,1)S(1)}, u32[]{:S(2)}, u32[]{:S(2)}) %collective-permute-start.13) | collective-permute-done | bytes 589856 | tf_op jit(solution)/shard_map/ppermute | solution.py:245
  322.7 12.7 %collective-permute-done.14 = bf16[1,192,768]{2,1,0:T(8,128)(2,1)S(1)} collective-permute-done((bf16[1,192,768]{2,1,0:T(8,128)(2,1)S(1)}, bf16[1,192,768]{2,1,0:T(8,128)(2,1)S(1)}, u32[]{:S(2)}, u32[]{:S(2)}) %collective-permute-start.14) | collective-permute-done | bytes 294944 | tf_op jit(solution)/shard_map/ppermute | solution.py:245
  337.0 1.2 convert_element_type.112
  (223 shorter events, 30.9 us)
Async XLA Ops:
  7.2 45.0 %copy-start = (bf16[1,768,768]{2,1,0:T(8,128)(2,1)S(1)}, bf16[1,768,768]{2,1,0:T(8,128)(2,1)}, u32[]{:S(2)}) copy-start(bf16[1,768,768]{2,1,0:T(8,128)(2,1)} %param.21) | copy-start | bytes 3538948
  7.2 9.4 %copy-start.52 = (s32[192]{0:T(256)S(1)}, s32[192]{0:T(256)}, u32[]{:S(2)}) copy-start(s32[192]{0:T(256)} %param.28) | copy-start | bytes 2308
  7.2 9.4 %slice-start = ((s32[192]{0:T(256)}), s32[6]{0:T(128)S(1)}, s32[]{:S(2)}) async-start(s32[192]{0:T(256)} %param.28), calls=%async_computation.2 | async-start | bytes 1024 | tf_op jit(solution)/shard_map/slice | solution.py:334
  7.2 9.4 %copy-start.49 = (f32[1,768,3]{1,0,2:T(1,128)S(1)}, f32[1,768,3]{1,0,2:T(1,128)}, u32[]{:S(2)}) copy-start(f32[1,768,3]{1,0,2:T(1,128)} %param.18) | copy-start | bytes 27652
  7.2 9.4 %copy-start.50 = (f32[1,768,3]{1,0,2:T(1,128)S(1)}, f32[1,768,3]{1,0,2:T(1,128)}, u32[]{:S(2)}) copy-start(f32[1,768,3]{1,0,2:T(1,128)} %param.17) | copy-start | bytes 27652
  7.2 329.7 %reduce-scatter.2.cloned.1.call-start = ((), (), s32[]{:S(2)}) async-start(), calls=%async_computation.1 | async-start | bytes 10027008 | tf_op jit(solution)/shard_map/reduce_scatter | solution.py:389
  8.6 14.2 %copy-start.34 = (bf16[288,768]{1,0:T(8,128)(2,1)}, bf16[288,768]{1,0:T(8,128)(2,1)S(1)}, u32[]{:S(2)}) copy-start(bf16[288,768]{1,0:T(8,128)(2,1)S(1)} %get-tuple-element.166) | copy-start | bytes 1327108
  8.6 13.1 %collective-permute-start = (bf16[288,768]{1,0:T(8,128)(2,1)S(1)}, bf16[288,768]{1,0:T(8,128)(2,1)S(1)}, u32[]{:S(2)}, u32[]{:S(2)}) collective-permute-start(bf16[288,768]{1,0:T(8,128)(2,1)S(1)} %get-tuple-element.167), channel_id=1, source_target_pairs={{1,0},{2,1},{3,2},{4,3},{5,4},{6,5},{7,6},{8,7},{9,8},{10,9},{11,1... | collective-permute-start | bytes 1327112 | tf_op jit(solution)/shard_map/ppermute | solution.py:348
  16.9 5.8 %copy-start.47 = (f32[768]{0:T(1024)}, f32[768]{0:T(1024)S(1)}, u32[]{:S(2)}) copy-start(f32[768]{0:T(1024)S(1)} %get-tuple-element.200) | copy-start | bytes 9220
  21.7 2.2 copy-start.53
  27.1 10.6 %copy-start.4 = (bf16[576,2304]{1,0:T(8,128)(2,1)}, bf16[576,2304]{1,0:T(8,128)(2,1)S(1)}, u32[]{:S(2)}) copy-start(bf16[576,2304]{1,0:T(8,128)(2,1)S(1)} %convolution_convert_fusion.q_ref.k_ref.v_ref) | copy-start | bytes 7962628
  27.1 23.3 %copy-start.57 = (bf16[1,768,768]{2,1,0:T(8,128)(2,1)S(1)}, bf16[1,768,768]{2,1,0:T(8,128)(2,1)}, u32[]{:S(2)}) copy-start(bf16[1,768,768]{2,1,0:T(8,128)(2,1)} %param.20) | copy-start | bytes 3538948
  37.6 13.7 %copy-start.11 = (bf16[576,768]{1,0:T(8,128)(2,1)}, bf16[576,768]{1,0:T(8,128)(2,1)S(1)}, u32[]{:S(2)}) copy-start(bf16[576,768]{1,0:T(8,128)(2,1)S(1)} %get-tuple-element.44.x_ref) | copy-start | bytes 2654212
  37.6 13.7 %copy-start.23 = (f32[6,2,576]{2,1,0:T(2,128)}, f32[6,2,576]{2,1,0:T(2,128)S(1)}, u32[]{:S(2)}) copy-start(f32[6,2,576]{2,1,0:T(2,128)S(1)} %get-tuple-element.60.lse_ref) | copy-start | bytes 82948
  37.6 12.7 %copy-start.46 = (bf16[1,576,768]{2,1,0:T(8,128)(2,1)S(1)}, bf16[1,576,768]{2,1,0:T(8,128)(2,1)}, u32[]{:S(2)}) copy-start(bf16[1,576,768]{2,1,0:T(8,128)(2,1)} %param.15) | copy-start | bytes 2654212
  37.7 12.6 %collective-permute-start.1 = (bf16[288,768]{1,0:T(8,128)(2,1)S(1)}, bf16[288,768]{1,0:T(8,128)(2,1)S(1)}, u32[]{:S(2)}, u32[]{:S(2)}) collective-permute-start(bf16[288,768]{1,0:T(8,128)(2,1)S(1)} %get-tuple-element.164), channel_id=1, source_target_pairs={{0,1},{1,2},{2,3},{3,4},{4,5},{5,6},{6,7},{7,8},{8,9},{9,10},{10,1... | collective-permute-start | bytes 1327112 | tf_op jit(solution)/shard_map/ppermute | solution.py:351
  51.3 27.1 %copy-start.32 = (f32[576,768]{1,0:T(8,128)}, f32[576,768]{1,0:T(8,128)S(1)}, u32[]{:S(2)}) copy-start(f32[576,768]{1,0:T(8,128)S(1)} %get-tuple-element.190) | copy-start | bytes 5308420
  52.1 14.1 %copy-start.55 = (bf16[1,768,1536]{2,1,0:T(8,128)(2,1)S(1)}, bf16[1,768,1536]{2,1,0:T(8,128)(2,1)}, u32[]{:S(2)}) copy-start(bf16[1,768,1536]{2,1,0:T(8,128)(2,1)} %param.22) | copy-start | bytes 7077892
  52.1 14.1 %collective-permute-start.2 = (bf16[576,768]{1,0:T(8,128)(2,1)S(1)}, bf16[576,768]{1,0:T(8,128)(2,1)S(1)}, u32[]{:S(2)}, u32[]{:S(2)}) collective-permute-start(bf16[576,768]{1,0:T(8,128)(2,1)S(1)} %add_convert_fusion.4.x_ref), channel_id=1, source_target_pairs={{0,16},{16,0},{1,17},{17,1},{2,18},{18,2},{3,19},{19,3},{4,20},{20... | collective-permute-start | bytes 2654216 | tf_op jit(solution)/shard_map/ppermute | solution.py:354
  53.0 14.7 %copy-start.28 = (bf16[576,768]{1,0:T(8,128)(2,1)}, bf16[576,768]{1,0:T(8,128)(2,1)S(1)}, u32[]{:S(2)}) copy-start(bf16[576,768]{1,0:T(8,128)(2,1)S(1)} %convolution_convert_fusion.4.q_ref) | copy-start | bytes 2654212
  67.7 10.7 %copy-start.26 = (bf16[576,1536]{1,0:T(8,128)(2,1)}, bf16[576,1536]{1,0:T(8,128)(2,1)S(1)}, u32[]{:S(2)}) copy-start(bf16[576,1536]{1,0:T(8,128)(2,1)S(1)} %convolution_convert_fusion.1.k_ref.v_ref) | copy-start | bytes 5308420
  67.7 10.7 %copy-start.45 = (bf16[1,768,768]{2,1,0:T(8,128)(2,1)S(1)}, bf16[1,768,768]{2,1,0:T(8,128)(2,1)}, u32[]{:S(2)}) copy-start(bf16[1,768,768]{2,1,0:T(8,128)(2,1)} %param.23) | copy-start | bytes 3538948
  67.8 12.4 %slice-start.1 = ((s8[4718592]{0:T(1024)(128)(4,1)}), s8[4194304]{0:T(1024)(128)(4,1)S(1)}, s32[]{:S(2)}) async-start(s8[4718592]{0:T(1024)(128)(4,1)} %bitcast.155), calls=%async_computation.3 | async-start | bytes 8388608
  79.4 20.9 %copy-start.30 = (f32[576,768]{1,0:T(8,128)}, f32[576,768]{1,0:T(8,128)S(1)}, u32[]{:S(2)}) copy-start(f32[576,768]{1,0:T(8,128)S(1)} %get-tuple-element.192) | copy-start | bytes 5308420
  79.8 7.2 %slice-start.3 = ((s8[4718592]{0:T(1024)(128)(4,1)}), s8[4194304]{0:T(1024)(128)(4,1)S(1)}, s32[]{:S(2)}) async-start(s8[4718592]{0:T(1024)(128)(4,1)} %bitcast.157), calls=%async_computation.5 | async-start | bytes 8388608
  80.6 6.5 %copy-start.10 = (bf16[1,576,768]{2,1,0:T(8,128)(2,1)S(1)}, bf16[1,576,768]{2,1,0:T(8,128)(2,1)}, u32[]{:S(2)}) copy-start(bf16[1,576,768]{2,1,0:T(8,128)(2,1)} %param.16) | copy-start | bytes 2654212
  80.6 6.5 %slice-start.4 = ((s8[4718592]{0:T(1024)(128)(4,1)}), s8[524288]{0:T(1024)(128)(4,1)S(1)}, s32[]{:S(2)}) async-start(s8[4718592]{0:T(1024)(128)(4,1)} %bitcast.157), calls=%async_computation.6 | async-start | bytes 1048576
  87.1 17.1 %copy-start.8 = (bf16[576,3072]{1,0:T(8,128)(2,1)}, bf16[576,3072]{1,0:T(8,128)(2,1)S(1)}, u32[]{:S(2)}) copy-start(bf16[576,3072]{1,0:T(8,128)(2,1)S(1)} %get-tuple-element.193.x_ref) | copy-start | bytes 10616836
  115.9 3.6 %copy-start.1 = (bf16[16,384,768]{2,1,0:T(8,128)(2,1)}, bf16[16,384,768]{2,1,0:T(8,128)(2,1)S(1)}, u32[]{:S(2)}) copy-start(bf16[16,384,768]{2,1,0:T(8,128)(2,1)S(1)} %gup.1) | copy-start | bytes 28311556
  123.4 16.2 %copy-start.56 = (bf16[1,768,1536]{2,1,0:T(8,128)(2,1)S(1)}, bf16[1,768,1536]{2,1,0:T(8,128)(2,1)}, u32[]{:S(2)}) copy-start(bf16[1,768,1536]{2,1,0:T(8,128)(2,1)} %param.22) | copy-start | bytes 7077892
  142.9 13.9 %collective-permute-start.3 = (bf16[576,768]{1,0:T(8,128)(2,1)}, bf16[576,768]{1,0:T(8,128)(2,1)}, u32[]{:S(2)}, u32[]{:S(2)}) collective-permute-start(bf16[576,768]{1,0:T(8,128)(2,1)} %add_convert_fusion.1), channel_id=1, source_target_pairs={{0,16},{16,0},{1,17},{17,1},{2,18},{18,2},{3,19},{19,3},{4,20},{20... | collective-permute-start | bytes 2654216 | tf_op jit(solution)/shard_map/ppermute | solution.py:354
  145.6 2.8 copy-start.16
  148.4 2.8 copy-start.20
  151.2 2.8 copy-start.18
  154.0 2.8 copy-start.33
  154.0 22.0 %slice-start.5 = ((s8[4718592]{0:T(1024)(128)(4,1)}), s8[4194304]{0:T(1024)(128)(4,1)S(1)}, s32[]{:S(2)}) async-start(s8[4718592]{0:T(1024)(128)(4,1)} %bitcast.159), calls=%async_computation.7 | async-start | bytes 8388608
  156.8 3.4 copy-start.2
  156.8 3.5 copy-start.38
  156.8 19.3 %slice-start.6 = ((s8[4718592]{0:T(1024)(128)(4,1)}), s8[524288]{0:T(1024)(128)(4,1)S(1)}, s32[]{:S(2)}) async-start(s8[4718592]{0:T(1024)(128)(4,1)} %bitcast.159), calls=%async_computation.8 | async-start | bytes 1048576
  156.8 40.3 %collective-permute-start.5 = (bf16[8,192,768]{2,1,0:T(8,128)(2,1)}, bf16[8,192,768]{2,1,0:T(8,128)(2,1)}, u32[]{:S(2)}, u32[]{:S(2)}) collective-permute-start(bf16[8,192,768]{2,1,0:T(8,128)(2,1)} %get-tuple-element.58), channel_id=1, source_target_pairs={{0,1},{1,0},{2,3},{3,2},{4,5},{5,4},{6,7},{7,6},{8,9},{9,8},{10,11... | collective-permute-start | bytes 7077896 | tf_op jit(solution)/shard_map/ppermute | solution.py:245
  160.3 15.8 %copy-start.9 = (bf16[576,3072]{1,0:T(8,128)(2,1)S(1)}, bf16[576,3072]{1,0:T(8,128)(2,1)}, u32[]{:S(2)}) copy-start(bf16[576,3072]{1,0:T(8,128)(2,1)} %copy-done.8) | copy-start | bytes 10616836
  160.9 15.2 %copy-start.31 = (f32[576,768]{1,0:T(8,128)S(1)}, f32[576,768]{1,0:T(8,128)}, u32[]{:S(2)}) copy-start(f32[576,768]{1,0:T(8,128)} %copy-done.30) | copy-start | bytes 5308420
  160.9 30.4 %copy-start.40 = (bf16[288,768]{1,0:T(8,128)(2,1)}, bf16[288,768]{1,0:T(8,128)(2,1)S(1)}, u32[]{:S(2)}) copy-start(bf16[288,768]{1,0:T(8,128)(2,1)S(1)} %get-tuple-element.162) | copy-start | bytes 1327108
  161.0 30.4 %collective-permute-start.4 = (bf16[288,768]{1,0:T(8,128)(2,1)S(1)}, bf16[288,768]{1,0:T(8,128)(2,1)S(1)}, u32[]{:S(2)}, u32[]{:S(2)}) collective-permute-start(bf16[288,768]{1,0:T(8,128)(2,1)S(1)} %get-tuple-element.163), channel_id=1, source_target_pairs={{1,0},{2,1},{3,2},{4,3},{5,4},{6,5},{7,6},{8,7},{9,8},{10,9},{11,1... | collective-permute-start | bytes 1327112 | tf_op jit(solution)/shard_map/ppermute | solution.py:348
  192.1 4.1 %copy-start.58 = (bf16[1,768,768]{2,1,0:T(8,128)(2,1)S(1)}, bf16[1,768,768]{2,1,0:T(8,128)(2,1)}, u32[]{:S(2)}) copy-start(bf16[1,768,768]{2,1,0:T(8,128)(2,1)} %param.20) | copy-start | bytes 3538948
  193.4 2.8 copy-start.41
  193.4 2.8 copy-start.44
  197.9 3.6 %copy-start.5 = (bf16[576,2304]{1,0:T(8,128)(2,1)S(1)}, bf16[576,2304]{1,0:T(8,128)(2,1)}, u32[]{:S(2)}) copy-start(bf16[576,2304]{1,0:T(8,128)(2,1)} %copy-done.4) | copy-start | bytes 7962628
  197.9 3.6 %copy-start.24 = (f32[6,2,576]{2,1,0:T(2,128)S(1)}, f32[6,2,576]{2,1,0:T(2,128)}, u32[]{:S(2)}) copy-start(f32[6,2,576]{2,1,0:T(2,128)} %copy-done.23) | copy-start | bytes 82948
  201.5 16.3 %copy-start.7 = (bf16[576,768]{1,0:T(8,128)(2,1)S(1)}, bf16[576,768]{1,0:T(8,128)(2,1)}, u32[]{:S(2)}) copy-start(bf16[576,768]{1,0:T(8,128)(2,1)} %copy-done.6) | copy-start | bytes 2654212
  223.3 2.8 copy-start.54
  226.1 29.8 %collective-permute-start.11 = (bf16[8,192,768]{2,1,0:T(8,128)(2,1)}, bf16[8,192,768]{2,1,0:T(8,128)(2,1)}, u32[]{:S(2)}, u32[]{:S(2)}) collective-permute-start(bf16[8,192,768]{2,1,0:T(8,128)(2,1)} %get-tuple-element.71), channel_id=1, source_target_pairs={{0,1},{1,0},{2,3},{3,2},{4,5},{5,4},{6,7},{7,6},{8,9},{9,8},{10,11... | collective-permute-start | bytes 7077896 | tf_op jit(solution)/shard_map/ppermute | solution.py:245
  235.9 1.4 collective-permute-start.7
  240.1 9.0 %collective-permute-start.8 = (f32[4,528]{1,0:T(4,128)S(1)}, f32[4,528]{1,0:T(4,128)S(1)}, u32[]{:S(2)}, u32[]{:S(2)}) collective-permute-start(f32[4,528]{1,0:T(4,128)S(1)} %bitcast.153), channel_id=1, source_target_pairs={{0,2},{1,3},{2,0},{3,1},{4,6},{5,7},{6,4},{7,5},{8,10},{9,11},{10,... | collective-permute-start | bytes 25352 | tf_op jit(solution)/shard_map/ppermute | solution.py:245
  248.7 29.2 %collective-permute-start.15 = (bf16[4,192,768]{2,1,0:T(8,128)(2,1)}, bf16[4,192,768]{2,1,0:T(8,128)(2,1)}, u32[]{:S(2)}, u32[]{:S(2)}) collective-permute-start(bf16[4,192,768]{2,1,0:T(8,128)(2,1)} %get-tuple-element.73), channel_id=1, source_target_pairs={{0,2},{1,3},{2,0},{3,1},{4,6},{5,7},{6,4},{7,5},{8,10},{9,11},{10,... | collective-permute-start | bytes 3538952 | tf_op jit(solution)/shard_map/ppermute | solution.py:245
  251.8 3.7 %collective-permute-start.9 = (f32[2,528]{1,0:T(2,128)S(1)}, f32[2,528]{1,0:T(2,128)S(1)}, u32[]{:S(2)}, u32[]{:S(2)}) collective-permute-start(f32[2,528]{1,0:T(2,128)S(1)} %bitcast.154), channel_id=1, source_target_pairs={{0,4},{1,5},{2,6},{3,7},{4,0},{5,1},{6,2},{7,3},{8,12},{9,13},{10,... | collective-permute-start | bytes 12680 | tf_op jit(solution)/shard_map/ppermute | solution.py:245
  255.5 26.3 %collective-permute-start.10 = (f32[1,528]{1,0:T(1,128)S(1)}, f32[1,528]{1,0:T(1,128)S(1)}, u32[]{:S(2)}, u32[]{:S(2)}) collective-permute-start(f32[1,528]{1,0:T(1,128)S(1)} %constant_dynamic-slice_fusion), channel_id=1, source_target_pairs={{0,8},{1,9},{2,10},{3,11},{4,12},{5,13},{6,14},{7,15},{8,0},{9,1},... | collective-permute-start | bytes 6344 | tf_op jit(solution)/shard_map/ppermute | solution.py:245
  255.9 22.0 %copy-start.39 = (bf16[4,192,768]{2,1,0:T(8,128)(2,1)S(1)}, bf16[4,192,768]{2,1,0:T(8,128)(2,1)}, u32[]{:S(2)}) copy-start(bf16[4,192,768]{2,1,0:T(8,128)(2,1)} %get-tuple-element.72) | copy-start | bytes 3538948
  257.9 48.7 %collective-permute-start.12 = (bf16[4,192,768]{2,1,0:T(8,128)(2,1)S(1)}, bf16[4,192,768]{2,1,0:T(8,128)(2,1)S(1)}, u32[]{:S(2)}, u32[]{:S(2)}) collective-permute-start(bf16[4,192,768]{2,1,0:T(8,128)(2,1)S(1)} %get-tuple-element.148), channel_id=1, source_target_pairs={{0,2},{1,3},{2,0},{3,1},{4,6},{5,7},{6,4},{7,5},{8,10},{9,11},{10,... | collective-permute-start | bytes 3538952 | tf_op jit(solution)/shard_map/ppermute | solution.py:245
  279.3 13.2 %collective-permute-start.16 = (bf16[2,192,768]{2,1,0:T(8,128)(2,1)S(1)}, bf16[2,192,768]{2,1,0:T(8,128)(2,1)S(1)}, u32[]{:S(2)}, u32[]{:S(2)}) collective-permute-start(bf16[2,192,768]{2,1,0:T(8,128)(2,1)S(1)} %get-tuple-element.152), channel_id=1, source_target_pairs={{0,4},{1,5},{2,6},{3,7},{4,0},{5,1},{6,2},{7,3},{8,12},{9,13},{10,... | collective-permute-start | bytes 1769480 | tf_op jit(solution)/shard_map/ppermute | solution.py:245
  279.9 29.3 %collective-permute-start.6 = (bf16[288,768]{1,0:T(8,128)(2,1)S(1)}, bf16[288,768]{1,0:T(8,128)(2,1)S(1)}, u32[]{:S(2)}, u32[]{:S(2)}) collective-permute-start(bf16[288,768]{1,0:T(8,128)(2,1)S(1)} %get-tuple-element.160), channel_id=1, source_target_pairs={{0,1},{1,2},{2,3},{3,4},{4,5},{5,6},{6,7},{7,8},{8,9},{9,10},{10,1... | collective-permute-start | bytes 1327112 | tf_op jit(solution)/shard_map/ppermute | solution.py:351
  292.5 17.6 %collective-permute-start.17 = (bf16[1,192,768]{2,1,0:T(8,128)(2,1)S(1)}, bf16[1,192,768]{2,1,0:T(8,128)(2,1)S(1)}, u32[]{:S(2)}, u32[]{:S(2)}) collective-permute-start(bf16[1,192,768]{2,1,0:T(8,128)(2,1)S(1)} %slice_add_fusion.8), channel_id=1, source_target_pairs={{0,8},{1,9},{2,10},{3,11},{4,12},{5,13},{6,14},{7,15},{8,0},{9,1},... | collective-permute-start | bytes 884744 | tf_op jit(solution)/shard_map/ppermute | solution.py:245
  306.8 14.3 %collective-permute-start.13 = (bf16[2,192,768]{2,1,0:T(8,128)(2,1)S(1)}, bf16[2,192,768]{2,1,0:T(8,128)(2,1)S(1)}, u32[]{:S(2)}, u32[]{:S(2)}) collective-permute-start(bf16[2,192,768]{2,1,0:T(8,128)(2,1)S(1)} %get-tuple-element.154), channel_id=1, source_target_pairs={{0,4},{1,5},{2,6},{3,7},{4,0},{5,1},{6,2},{7,3},{8,12},{9,13},{10,... | collective-permute-start | bytes 1769480 | tf_op jit(solution)/shard_map/ppermute | solution.py:245
  321.2 14.2 %collective-permute-start.14 = (bf16[1,192,768]{2,1,0:T(8,128)(2,1)S(1)}, bf16[1,192,768]{2,1,0:T(8,128)(2,1)S(1)}, u32[]{:S(2)}, u32[]{:S(2)}) collective-permute-start(bf16[1,192,768]{2,1,0:T(8,128)(2,1)S(1)} %slice_add_fusion.10), channel_id=1, source_target_pairs={{0,8},{1,9},{2,10},{3,11},{4,12},{5,13},{6,14},{7,15},{8,0},{9,1},... | collective-permute-start | bytes 884744 | tf_op jit(solution)/shard_map/ppermute | solution.py:245
  (22 other events, 28.4 us)
Sparse Core Ops, SparseCore 0:
  119.7 117.6 reduce-scatter.1
